TPU v7x, 128 devices: a whole 4x4x4 slice. The times are simulated.
128 devices in a mesh: gx: 8 (over z_hi, x), gy: 16 (over z_lo, y, core).
Axes of the slice: x: 4, y: 4, z: 4 (z_hi: 2, z_lo: 2; z = z_hi * 2 + z_lo), core: 2. Of those that a mesh axis runs over, the one named last changes fastest.
Arguments:
- tracers: float32 [2, 8, 1024, 2048], P(None, None, 'gy', 'gx'), may hold values from -6 to 6
- east_speed: float32 [8, 1024, 2048], P(None, 'gy', 'gx'), may hold values from -0.2 to 0.2
- north_speed: float32 [8, 1024, 2048], P(None, 'gy', 'gx'), may hold values from -0.2 to 0.2
- vertical_mix: float32 [7, 1024, 2048], P(None, 'gy', 'gx'), may hold values from 0.05 to 5
- level_count: int32 [1024, 2048], P('gy', 'gx'), may hold values from 0 to 8, as said below
- atmosphere_flux: float32 [8, 256, 1024], P(None, 'gy', 'gx'), may hold values from -6 to 6
- intersection_source: int32 [8192, 1024], P('gy', 'gx'), may hold values from 0 to 2047, as said below
- intersection_target: int32 [8192, 1024], P('gy', 'gx'), may hold values from 0 to 16383, as said below
- intersection_weight: float32 [8192, 1024], P('gy', 'gx'), may hold values from 0 to 1, as said below
Outputs:
- tracers_out: float32 [2, 8, 1024, 2048], P(None, None, 'gy', 'gx')
- surface_flux: float32 [8, 1024, 2048], P(None, 'gy', 'gx')
Inputs may be any that keep to these rules, and one draw needn't show every extreme that they name: `intersection_source`: the slot from one atmosphere tile to one ocean tile of the same longitude tile has 4096 entries, live entries first. A slot from latitude tile s to latitude tile d holds live entries only where |d - s| <= 1, or where d >= 14 and s >= 7; every such slot has at least one; other slots are all padding. Padded entries have source cell 0, target cell 0 and weight 0. `intersection_target`: padded entries name cell 0. `intersection_weight`: zero on padded entries, positive on live ones. `level_count`: 0 marks land.
All inputs are finite; a program needn't handle non-finite values.
Results may differ from a plain program's by a relative error of at most 0.0003.
Values sent between devices are 32-bit elements; how exact they have to be, the bound alone decides.
No kernel may reach another device: no remote copies, remote signals or barrier semaphores. Data moves between devices by JAX's collectives and lax.ppermute only.
A program may use at most 64 MiB of HBM per device.

v0:
```python
import functools

import jax
import jax.numpy as jnp
from jax import lax
from jax.experimental import pallas as pl
from jax.experimental.pallas import tpu as pltpu
from jax.sharding import PartitionSpec as P

DIFFUSE = 0.05
FIELDS = 8
TRACERS = 2
NZ = 8
ROWS = 64
COLUMNS = 256
LANES = 128
GX = 8
GY = 16
SLOT_ROWS = 32
ATMOS_ROWS = 16
HELPED_BY = {12: GY - 2, 11: GY - 1}
DENSE = ((12, GY - 2), (11, GY - 1))
SENT_AWAY = 13
ENTRY_STEPS = (
    ((7, GY - 2), (8, GY - 1), (10, 12), (9, 11)),
    ((8, GY - 2), (7, GY - 1)),
    ((9, GY - 2), (13, GY - 1)),
)
CHANNELS = TRACERS * NZ
COUNT_AT = 24
RIM = 32
LIST = 3 * SLOT_ROWS
ATMOS = FIELDS * ATMOS_ROWS
PAYLOAD = LIST + ATMOS
CHUNK_ROWS = 16
CHUNK = CHUNK_ROWS * LANES
VMEM_LIMIT = 48 * 1024 * 1024
PACK_LIMIT = 63 * 1024 * 1024
F32 = jnp.float32
BF16 = jnp.bfloat16
F8 = jnp.float8_e4m3fn
LOW_TOP = 65536.0


def call(
    kernel, out_shapes, operands, scratch=(), flops=0, moved=4_000_000, in_hbm=False, out_hbm=False
):
    place = pltpu.HBM if in_hbm else pltpu.VMEM
    out_place = pl.ANY if out_hbm else pltpu.VMEM
    return pl.pallas_call(
        kernel,
        out_shape=[jax.ShapeDtypeStruct(shape, F32) for shape in out_shapes],
        in_specs=[pl.BlockSpec(memory_space=place) for _ in operands],
        out_specs=[pl.BlockSpec(memory_space=out_place) for _ in out_shapes],
        scratch_shapes=list(scratch),
        compiler_params=pltpu.CompilerParams(vmem_limit_bytes=PACK_LIMIT if in_hbm else VMEM_LIMIT),
        cost_estimate=pl.CostEstimate(flops=flops, bytes_accessed=moved, transcendentals=0),
    )(*operands)


def pack_columns(pick, channels, out_ref):
    lane = lax.broadcasted_iota(jnp.int32, (8, LANES), 1)
    for block in range(ROWS // 8):
        tile = jnp.zeros((8, LANES), F32)
        for channel in channels:
            value, at = pick(channel, block * 8)
            shift = (channel - at) % LANES
            moved = pltpu.roll(value, shift, axis=1) if shift else value
            tile = jnp.where(lane == channel, moved, tile)
        out_ref[pl.ds(block * 8, 8), :] = tile


def pack_row(value, channel, out_ref):
    out_ref[pl.ds(channel, 1), :] = value[:, :LANES]
    out_ref[pl.ds(RIM + channel, 1), :] = value[:, LANES:]


def is_even():
    return lax.rem(lax.axis_index("gy"), 2) == 0


def pack_rows(top_of, bottom_of, channels, sibling_ref, other_ref):
    even = is_even()
    zeros = jnp.zeros((2 * RIM, LANES), F32)
    sibling_ref[0 : 2 * RIM, :] = zeros
    other_ref[0 : 2 * RIM, :] = zeros
    for channel in channels:
        top, bottom = top_of(channel), bottom_of(channel)
        pack_row(jnp.where(even, top, bottom), channel, sibling_ref)
        pack_row(jnp.where(even, bottom, top), channel, other_ref)


def chosen(here, table, default):
    for key, value in table.items():
        default = jnp.where(here == key, value, default)
    return default


def among(here, table):
    return functools.reduce(jnp.logical_or, [here == key for key in table])


def list_into(lists, out_ref, at, tile, valid=None):
    rows = pl.ds(pl.multiple_of(tile * SLOT_ROWS, SLOT_ROWS), SLOT_ROWS)
    for kind, ref in enumerate(lists):
        part = ref[rows, :].astype(F32)
        if kind == 2 and valid is not None:
            part = jnp.where(valid, part, 0.0)
        out_ref[at + kind * SLOT_ROWS : at + (kind + 1) * SLOT_ROWS, :] = part


def pack_kernel(*refs):
    steps = len(ENTRY_STEPS)
    froms, refs = refs[:8], refs[8:]
    (to_east_ref, to_west_ref, sibling_ref, other_ref), refs = refs[:4], refs[4:]
    entry_refs, intos, (cells_ref, sems) = refs[:steps], refs[steps:-2], refs[-2:]
    tracers_ref, east_ref, north_ref, count_ref, source_ref, target_ref, weight_ref, atmos_ref = intos
    copies = [
        pltpu.make_async_copy(array, into, sems.at[n])
        for n, (array, into) in enumerate(zip(froms, intos, strict=True))
    ]
    for copy in copies:
        copy.start()
    for copy in copies[4:]:
        copy.wait()
    here = lax.axis_index("gy")
    even = is_even()
    lists = (source_ref, target_ref, weight_ref)
    for field in range(FIELDS):
        for row in range(ATMOS_ROWS):
            to = row * FIELDS + field
            cells_ref[to : to + 1, :] = atmos_ref[field, row : row + 1, :]
    cells = cells_ref[...]
    for pairs, out_ref in zip(ENTRY_STEPS, entry_refs, strict=True):
        wanted = {source: HELPED_BY.get(to, to) for source, to in pairs}
        list_into(lists, out_ref, 0, chosen(here, wanted, here))
        out_ref[LIST:PAYLOAD, :] = cells
    partner = here ^ 1
    list_into(lists, sibling_ref, 2 * RIM, chosen(partner, HELPED_BY, partner))
    list_into(lists, sibling_ref, 2 * RIM + LIST, partner, among(partner, HELPED_BY))
    sibling_ref[2 * RIM + 2 * LIST :, :] = cells
    away = jnp.clip(jnp.where(even, here - 1, here + 1), 0, GY - 1)
    below_top = here != GY - 1
    helped = jnp.logical_and(below_top, among(away, HELPED_BY))
    list_into(lists, other_ref, 2 * RIM, chosen(away, HELPED_BY, away), helped)
    direct = jnp.logical_and(below_top, here != SENT_AWAY)
    list_into(lists, other_ref, 2 * RIM + LIST, away, direct)
    other_ref[2 * RIM + 2 * LIST :, :] = cells

    for copy in copies[:4]:
        copy.wait()

    def east_column(channel, row):
        rows = pl.ds(row, 8)
        if channel < CHANNELS:
            return tracers_ref[channel, rows, LANES:], LANES - 1
        if channel < COUNT_AT:
            return east_ref[channel - CHANNELS, rows, LANES:], LANES - 1
        return count_ref[rows, LANES:].astype(F32), LANES - 1

    def west_column(channel, row):
        rows = pl.ds(row, 8)
        if channel < CHANNELS:
            return tracers_ref[channel, rows, :LANES], 0
        return count_ref[rows, :LANES].astype(F32), 0

    pack_columns(east_column, [*range(CHANNELS + NZ), COUNT_AT], to_east_ref)
    pack_columns(west_column, [*range(CHANNELS), COUNT_AT], to_west_ref)

    def top_of(channel):
        if channel < CHANNELS:
            return tracers_ref[channel, ROWS - 1 : ROWS, :]
        if channel < COUNT_AT:
            return north_ref[channel - CHANNELS, ROWS - 1 : ROWS, :]
        return count_ref[ROWS - 1 : ROWS, :].astype(F32)

    def bottom_of(channel):
        if channel < CHANNELS:
            return tracers_ref[channel, 0:1, :]
        if channel < COUNT_AT:
            return jnp.zeros((1, COLUMNS), F32)
        return count_ref[0:1, :].astype(F32)

    pack_rows(top_of, bottom_of, range(COUNT_AT + 1), sibling_ref, other_ref)


def step_kernel(
    forced,
    q_ref,
    from_west_ref,
    from_east_ref,
    from_sibling_ref,
    from_other_ref,
    static_west_ref,
    static_east_ref,
    static_sibling_ref,
    static_other_ref,
    east_ref,
    north_ref,
    count_ref,
    mix_ref,
    *more_refs,
):
    if forced:
        out_ref, gain_ref = more_refs[-6:-4]
    else:
        forcing_ref, out_hbm, out_ref, sems = more_refs[:4]
    from_south_ref, top_ref, static_south_ref, static_top_ref = more_refs[-4:]
    even = is_even()
    on_top = lax.axis_index("gy") == GY - 1
    lane = lax.broadcasted_iota(jnp.int32, (8, LANES), 1)
    row = lax.broadcasted_iota(jnp.int32, (8, LANES), 0)
    first_lane, last_lane = lane == 0, lane == LANES - 1
    first_row, last_row = row == 0, row == 7

    def set_rims(sibling_rim, other_rim, south, north):
        @pl.when(even)
        def _():
            south[...] = other_rim[0 : 2 * RIM, :]
            north[...] = sibling_rim[0 : 2 * RIM, :]

        @pl.when(jnp.logical_not(even))
        def _():
            south[...] = sibling_rim[0 : 2 * RIM, :]
            north[...] = other_rim[0 : 2 * RIM, :]

        @pl.when(on_top)
        def _():
            flipped = LANES - 1 - lane
            for half in range(2):
                for block in range(RIM // 8):
                    rows = other_rim[pl.ds((1 - half) * RIM + block * 8, 8), :]
                    north[pl.ds(half * RIM + block * 8, 8), :] = jnp.take_along_axis(
                        rows, flipped, axis=1, mode="promise_in_bounds"
                    )

    set_rims(from_sibling_ref, from_other_ref, from_south_ref, top_ref)
    set_rims(static_sibling_ref, static_other_ref, static_south_ref, static_top_ref)

    def block_step(block, carry):
        at = pl.multiple_of(block * 8, 8)
        below = pl.multiple_of(jnp.maximum(block - 1, 0) * 8, 8)
        above = pl.multiple_of(jnp.minimum(block + 1, ROWS // 8 - 1) * 8, 8)
        is_first, is_last = block == 0, block == ROWS // 8 - 1
        rows = pl.ds(at, 8)

        def halves(load):
            return [load(rows, slice(0, LANES)), load(rows, slice(LANES, 2 * LANES))]

        def to_west_of(parts, rim):
            low = jnp.where(last_lane, rim, parts[0])
            high = jnp.where(last_lane, parts[0], parts[1])
            return [pltpu.roll(low, 1, axis=1), pltpu.roll(high, 1, axis=1)]

        def to_east_of(parts, rim):
            low = jnp.where(first_lane, parts[1], parts[0])
            high = jnp.where(first_lane, rim, parts[1])
            return [
                pltpu.roll(low, LANES - 1, axis=1),
                pltpu.roll(high, LANES - 1, axis=1),
            ]

        def to_south_of(load, parts, rim_ref, channel):
            found = []
            for half in range(2):
                lanes = slice(half * LANES, (half + 1) * LANES)
                rim = jnp.broadcast_to(
                    rim_ref[half * RIM + channel : half * RIM + channel + 1, :], (8, LANES)
                )
                near = jnp.where(is_first, rim, load(pl.ds(below, 8), lanes))
                found.append(pltpu.roll(jnp.where(last_row, near, parts[half]), 1, axis=0))
            return found

        def to_north_of(load, parts, rim_ref, channel):
            found = []
            for half in range(2):
                lanes = slice(half * LANES, (half + 1) * LANES)
                rim = jnp.broadcast_to(
                    rim_ref[half * RIM + channel : half * RIM + channel + 1, :], (8, LANES)
                )
                near = jnp.where(is_last, rim, load(pl.ds(above, 8), lanes))
                found.append(pltpu.roll(jnp.where(first_row, near, parts[half]), 7, axis=0))
            return found

        def west_rim(ref, channel):
            return pltpu.roll(ref[rows, :], (LANES - 1 - channel) % LANES, axis=1)

        def east_rim(ref, channel):
            shift = (LANES - channel) % LANES
            return pltpu.roll(ref[rows, :], shift, axis=1) if shift else ref[rows, :]

        def load_count(where, lanes):
            return count_ref[where, lanes].astype(F32)

        count = halves(load_count)
        sides = [
            to_east_of(count, east_rim(static_east_ref, COUNT_AT)),
            to_west_of(count, west_rim(static_west_ref, COUNT_AT)),
            to_north_of(load_count, count, static_top_ref, COUNT_AT),
            to_south_of(load_count, count, static_south_ref, COUNT_AT),
        ]
        shared = [[jnp.minimum(count[half], side[half]) for half in range(2)] for side in sides]
        closed = jnp.logical_and(jnp.logical_and(on_top, is_last), last_row)

        values = [[[None, None] for _ in range(NZ)] for _ in range(TRACERS)]
        for level in range(NZ):
            east = halves(lambda where, lanes: east_ref[level, where, lanes])
            west = to_west_of(east, west_rim(static_west_ref, CHANNELS + level))

            def load_north(where, lanes):
                return north_ref[level, where, lanes]

            north = halves(load_north)
            south = to_south_of(load_north, north, static_south_ref, CHANNELS + level)
            coefs = []
            for half in range(2):
                limit = float(level)
                up = jnp.where(closed, 0.0, north[half])
                open_e, open_w, open_n, open_s = [side[half] > limit for side in shared]

                def into(opened, speed):
                    return jnp.where(opened, DIFFUSE - jnp.minimum(speed, 0.0), 0.0)

                def away(opened, speed):
                    return jnp.where(opened, DIFFUSE + jnp.maximum(speed, 0.0), 0.0)

                from_e, lost_e = into(open_e, east[half]), away(open_e, east[half])
                from_w, lost_w = away(open_w, west[half]), into(open_w, west[half])
                from_n, lost_n = into(open_n, up), away(open_n, up)
                from_s, lost_s = away(open_s, south[half]), into(open_s, south[half])
                kept = 1.0 - ((lost_e + lost_w) + (lost_n + lost_s))
                coefs.append((kept, from_e, from_w, from_n, from_s))
            for tracer in range(TRACERS):
                channel = tracer * NZ + level

                def load_q(where, lanes):
                    return q_ref[channel, where, lanes]

                q = halves(load_q)
                q_e = to_east_of(q, east_rim(from_east_ref, channel))
                q_w = to_west_of(q, west_rim(from_west_ref, channel))
                q_n = to_north_of(load_q, q, top_ref, channel)
                q_s = to_south_of(load_q, q, from_south_ref, channel)
                for half in range(2):
                    kept, from_e, from_w, from_n, from_s = coefs[half]
                    values[tracer][level][half] = (
                        kept * q[half]
                        + (from_e * q_e[half] + from_w * q_w[half])
                        + (from_n * q_n[half] + from_s * q_s[half])
                    )
        for half in range(2):
            lanes = slice(half * LANES, (half + 1) * LANES)
            sides_here = [[values[t][k][half] for k in range(NZ)] for t in range(TRACERS)]
            surface = count[half] > 0.0
            if forced:
                sides_here.append([jnp.where(surface, 1.0, 0.0)] + [None] * (NZ - 1))
            else:
                for tracer in range(TRACERS):
                    forcing = jnp.where(surface, forcing_ref[tracer, rows, lanes], 0.0)
                    sides_here[tracer][0] = sides_here[tracer][0] + forcing
            ratios = []
            partials = [[] for _ in sides_here]
            for level in range(NZ):
                thickness = 1.0 + level / NZ
                upper = lower = None
                if level >= 1:
                    mix = mix_ref[level - 1, rows, lanes]
                    upper = jnp.where(count[half] > float(level), mix * (1.0 / thickness), 0.0)
                if level <= NZ - 2:
                    mix = mix_ref[level, rows, lanes]
                    lower = jnp.where(
                        count[half] > float(level + 1), mix * (1.0 / thickness), 0.0
                    )
                if upper is None:
                    pivot = 1.0 + lower
                elif lower is None:
                    pivot = 1.0 + upper - upper * ratios[-1]
                else:
                    pivot = 1.0 + upper + lower - upper * ratios[-1]
                inverse = 1.0 / pivot
                if lower is not None:
                    ratios.append(lower * inverse)
                for side, partial in zip(sides_here, partials, strict=True):
                    right = side[level]
                    if level >= 1:
                        carried = upper * partial[-1]
                        right = carried if right is None else right + carried
                    partial.append(right * inverse)
            for index, partial in enumerate(partials):
                solved = partial[-1]
                for level in range(NZ - 1, -1, -1):
                    if level < NZ - 1:
                        solved = partial[level] + ratios[level] * solved
                    if index < TRACERS:
                        out_ref[index * NZ + level, rows, lanes] = solved
                    else:
                        gain_ref[level, rows, lanes] = solved
        if not forced:
            block_copy(block).start()
        return carry

    def block_copy(block):
        rows = pl.ds(pl.multiple_of(block * 8, 8), 8)
        return pltpu.make_async_copy(out_ref.at[:, rows, :], out_hbm.at[:, rows, :], sems.at[block])

    lax.fori_loop(0, ROWS // 8, block_step, 0)
    if not forced:
        for block in range(ROWS // 8):
            block_copy(block).wait()


def land_kernel(slots, own_slot, reset, *refs):
    operand_refs, refs = refs[:-9], refs[-9:]
    if own_slot:
        own, operand_refs = operand_refs[:4], operand_refs[4:]
    here = lax.axis_index("gy")
    helps = among(here, HELPED_BY)
    if reset is not None:
        start_ref = operand_refs[-1]
    total_ref, lists_ref, columns_ref, cells_ref = refs[:4]
    high_ref, low_ref, high_hot_ref, low_hot_ref, weights_ref = refs[4:]
    largest = jnp.zeros((8, LANES), F32)
    row_number = lax.broadcasted_iota(jnp.int32, (SLOT_ROWS, LANES), 0).astype(F32) + 1.0
    ends = []

    def unpack(slot):
        source, target, weight = weights_ref[0], weights_ref[1], weights_ref[2]
        rows = pl.ds(slot * SLOT_ROWS, SLOT_ROWS)
        source_row = jnp.floor(source * (1.0 / LANES))
        target_row = jnp.floor(target * (1.0 / COLUMNS))
        columns_ref[rows, :] = (source - source_row * LANES).astype(jnp.int32)
        lists_ref[0, rows, :] = source_row
        lists_ref[1, rows, :] = target_row
        lists_ref[2, rows, :] = target - target_row * COLUMNS
        lists_ref[3, rows, :] = weight
        return jnp.max(jnp.where(weight != 0.0, row_number, 0.0)).astype(jnp.int32)

    if own_slot:
        tile = here if reset else chosen(here, HELPED_BY, here)
        rows = pl.ds(pl.multiple_of(tile * SLOT_ROWS, SLOT_ROWS), SLOT_ROWS)
        for kind in range(3):
            part = own[kind][rows, :].astype(F32)
            if kind == 2 and reset:
                part = jnp.where(helps, part, 0.0)
            weights_ref[kind] = part
        ends.append(unpack(0))
        for field in range(FIELDS):
            largest = jnp.maximum(largest, jnp.abs(own[3][field, 0:8, :]))
            largest = jnp.maximum(largest, jnp.abs(own[3][field, 8:16, :]))
            for row in range(ATMOS_ROWS):
                cells_ref[0, row, field : field + 1, :] = own[3][field, row : row + 1, :]
    count = own_slot + len(slots)
    for slot, (operand, list_at, cells_at, only) in enumerate(slots, own_slot):
        ref = operand_refs[operand]
        for kind in range(3):
            rows = pl.ds(list_at + kind * SLOT_ROWS, SLOT_ROWS)
            part = ref[rows, :]
            if kind == 2 and only is not None:
                part = jnp.where(helps == only, part, 0.0)
            weights_ref[kind] = part
        ends.append(unpack(slot))
        for row in range(ATMOS_ROWS):
            cells = ref[pl.ds(cells_at + row * FIELDS, FIELDS), :]
            cells_ref[slot, row] = cells
            largest = jnp.maximum(largest, jnp.abs(cells))
    scale = LOW_TOP / jnp.maximum(jnp.max(largest), 1e-30)
    unscale = 1.0 / scale

    spare = count * SLOT_ROWS
    lists_ref[:, spare : spare + 8, :] = jnp.zeros((4, 8, LANES), F32)
    columns_ref[spare : spare + 8, :] = jnp.zeros((8, LANES), jnp.int32)
    firsts = [jnp.int32(0)]
    for end in ends:
        firsts.append(firsts[-1] + end)
    live = firsts.pop()

    def row_of(place):
        shift = jnp.int32(0)
        for slot in range(1, count):
            shift = jnp.where(place >= firsts[slot], slot * SLOT_ROWS - firsts[slot], shift)
        return jnp.where(place < live, place + shift, spare)

    if reset is None:
        total_ref[...] = jnp.zeros_like(total_ref)
    elif reset:

        @pl.when(helps)
        def _():
            total_ref[...] = jnp.zeros_like(total_ref)

        @pl.when(jnp.logical_not(helps))
        def _():
            total_ref[...] = start_ref[...]
    else:
        total_ref[...] = start_ref[...]
    ones, zeros = jnp.ones((), BF16), jnp.zeros((), BF16)
    iota = lax.broadcasted_iota(jnp.int32, (COLUMNS, LANES), 0).astype(F32).astype(BF16)

    def hot(values, height):
        line = jnp.broadcast_to(values, (16, LANES)).astype(BF16)
        return [jnp.where(line == iota[at : at + 16], ones, zeros) for at in range(0, height, 16)]

    def chunk(place, entries):
        for entry in range(entries):
            at = row_of(place + entry)
            one = pl.ds(at, 1)
            slot = jnp.minimum(lax.div(at, SLOT_ROWS), count - 1)
            lanes = slice(entry * LANES, (entry + 1) * LANES)
            row_here = jnp.broadcast_to(lists_ref[0, one, :], (FIELDS, LANES))
            column_here = jnp.broadcast_to(columns_ref[one, :], (FIELDS, LANES))
            picked = jnp.zeros((FIELDS, LANES), F32)
            for row in range(ATMOS_ROWS):
                found_here = jnp.take_along_axis(
                    cells_ref[slot, row], column_here, axis=1, mode="promise_in_bounds"
                )
                picked = jnp.where(row_here == float(row), found_here, picked)
            weighted = picked * lists_ref[3, one, :]
            high = weighted.astype(BF16).astype(F32)
            low = (weighted - high) * scale
            row_hot = hot(lists_ref[1, one, :], ROWS)
            for field in range(FIELDS):
                first = field * ROWS
                line = jnp.broadcast_to(high[field : field + 1, :], (16, LANES)).astype(BF16)
                for part in range(4):
                    high_ref[first + part * 16 : first + part * 16 + 16, lanes] = line * row_hot[part]
                line = jnp.broadcast_to(low[field : field + 1, :], (16, LANES)).astype(BF16)
                for part in range(2):
                    both = [line * row_hot[2 * part], line * row_hot[2 * part + 1]]
                    low_ref[first + part * 32 : first + part * 32 + 32, lanes] = jnp.concatenate(
                        both, axis=0
                    ).astype(F8)
            column_hot = hot(lists_ref[2, one, :], COLUMNS)
            for part in range(COLUMNS // 16):
                high_hot_ref[part * 16 : part * 16 + 16, lanes] = column_hot[part]
            for part in range(COLUMNS // 32):
                low_hot_ref[part * 32 : part * 32 + 32, lanes] = jnp.concatenate(
                    column_hot[2 * part : 2 * part + 2], axis=0
                ).astype(F8)
        over_entries = (((1,), (1,)), ((), ()))
        used = slice(0, entries * LANES)
        total_ref[...] += lax.dot_general(
            high_ref[:, used], high_hot_ref[:, used], over_entries, preferred_element_type=F32
        ) + unscale * lax.dot_general(
            low_ref[:, used], low_hot_ref[:, used], over_entries, preferred_element_type=F32
        )

    def chunk_step(at, carry):
        chunk(at * CHUNK_ROWS, CHUNK_ROWS)
        return carry

    half = CHUNK_ROWS // 2
    wholes = lax.div(live + (half - 1), CHUNK_ROWS)
    lax.fori_loop(0, wholes, chunk_step, 0)

    @pl.when(live > wholes * CHUNK_ROWS)
    def _():
        chunk(wholes * CHUNK_ROWS, half)


def finish_kernel(
    total_ref,
    helped_ref,
    solved_ref,
    gain_ref,
    result_ref,
    flux_ref,
    forcing_ref,
    to_east_ref,
    to_west_ref,
    sibling_ref,
    other_ref,
):
    def block_step(block, carry):
        rows = pl.ds(pl.multiple_of(block * 8, 8), 8)
        flux = []
        for field in range(FIELDS):
            from_rows = pl.ds(pl.multiple_of(field * ROWS + block * 8, 8), 8)
            value = total_ref[from_rows, :] + helped_ref[from_rows, :]
            flux_ref[field, rows, :] = value
            flux.append(value)
        heat = flux[0] + flux[1] + flux[2] + flux[3] + flux[4]
        salt = flux[7] - flux[5] - flux[6]
        forcing_ref[0, rows, :] = heat
        forcing_ref[1, rows, :] = salt
        for level in range(NZ):
            gain = gain_ref[level, rows, :]
            for tracer, forcing in enumerate((heat, salt)):
                channel = tracer * NZ + level
                result_ref[channel, rows, :] = solved_ref[channel, rows, :] + forcing * gain
        return carry

    lax.fori_loop(0, ROWS // 8, block_step, 0)
    pack_columns(
        lambda channel, row: (result_ref[channel, pl.ds(row, 8), LANES:], LANES - 1),
        range(CHANNELS),
        to_east_ref,
    )
    pack_columns(
        lambda channel, row: (result_ref[channel, pl.ds(row, 8), :LANES], 0),
        range(CHANNELS),
        to_west_ref,
    )
    pack_rows(
        lambda channel: result_ref[channel, ROWS - 1 : ROWS, :],
        lambda channel: result_ref[channel, 0:1, :],
        range(CHANNELS),
        sibling_ref,
        other_ref,
    )


EASTWARD = [(i, (i + 1) % GX) for i in range(GX)]
WESTWARD = [((i + 1) % GX, i) for i in range(GX)]
SIBLINGS = [(y, y ^ 1) for y in range(GY)]
OTHERS = [
    (x * GY + y, x * GY + (y + 1 if y % 2 else y - 1)) for x in range(GX) for y in range(1, GY - 1)
] + [(x * GY + GY - 1, (GX - 1 - x) * GY + GY - 1) for x in range(GX)]


def exchange(to_east, to_west, sibling, other):
    return (
        lax.ppermute(to_east, "gx", EASTWARD),
        lax.ppermute(to_west, "gx", WESTWARD),
        lax.ppermute(sibling, "gy", SIBLINGS),
        lax.ppermute(other, ("gx", "gy"), OTHERS),
    )


def land(operands, slots, own_slot, reset):
    count = own_slot + len(slots)
    (total,) = call(
        functools.partial(land_kernel, slots, own_slot, reset),
        [(FIELDS * ROWS, COLUMNS)],
        operands,
        [
            pltpu.VMEM((4, count * SLOT_ROWS + 8, LANES), F32),
            pltpu.VMEM((count * SLOT_ROWS + 8, LANES), jnp.int32),
            pltpu.VMEM((count, ATMOS_ROWS, FIELDS, LANES), F32),
            pltpu.VMEM((FIELDS * ROWS, CHUNK), BF16),
            pltpu.VMEM((FIELDS * ROWS, CHUNK), F8),
            pltpu.VMEM((COLUMNS, CHUNK), BF16),
            pltpu.VMEM((COLUMNS, CHUNK), F8),
            pltpu.VMEM((3, SLOT_ROWS, LANES), F32),
        ],
        moved=100_000,
    )
    return total


def local(
    tracers,
    east_speed,
    north_speed,
    vertical_mix,
    level_count,
    atmosphere_flux,
    intersection_source,
    intersection_target,
    intersection_weight,
):
    q = tracers.reshape(CHANNELS, ROWS, COLUMNS)
    statics = [east_speed, north_speed, level_count, vertical_mix]
    lists = [intersection_source, intersection_target, intersection_weight, atmosphere_flux]
    column_rim, row_rim = (ROWS, LANES), (2 * RIM, LANES)
    both = (2 * RIM + LIST + PAYLOAD, LANES)
    steps = len(ENTRY_STEPS)
    packed = call(
        pack_kernel,
        [column_rim, column_rim, both, both] + [(PAYLOAD, LANES)] * steps,
        [q, *statics[:3], *lists],
        [
            *[pltpu.VMEM(part.shape, part.dtype) for part in (q, *statics[:3], *lists)],
            pltpu.VMEM((ATMOS, LANES), F32),
            pltpu.SemaphoreType.DMA((8,)),
        ],
        in_hbm=True,
    )
    entries = [
        lax.ppermute(part, "gy", list(pairs))
        for part, pairs in zip(packed[4:], ENTRY_STEPS, strict=True)
    ]
    rims = exchange(*packed[:4])
    first, second, cells = 2 * RIM, 2 * RIM + LIST, 2 * RIM + 2 * LIST
    most = land([*lists, rims[2]], ((0, first, cells, None),), 1, None)
    partial = land(
        [rims[3], *entries, most], ((0, first, cells, None), (1, 0, LIST, True)), 0, False
    )
    helped = lax.ppermute(partial, "gy", list(DENSE))
    total = land(
        [*lists, rims[2], rims[3], *entries, partial],
        ((0, second, cells, None), (1, second, cells, None), (2, 0, LIST, False))
        + tuple((2 + step, 0, LIST, None) for step in range(1, steps)),
        1,
        True,
    )
    rim_scratch = [pltpu.VMEM(row_rim, F32)] * 4
    solved, gain = call(
        functools.partial(step_kernel, True),
        [q.shape, east_speed.shape],
        [q, *rims, *rims, *statics, partial],
        rim_scratch,
        moved=8_000_000,
    )
    result, flux, forcing, *out_rims = call(
        finish_kernel,
        [q.shape, (FIELDS, ROWS, COLUMNS), (TRACERS, ROWS, COLUMNS)]
        + [column_rim, column_rim, row_rim, row_rim],
        [total, helped, solved, gain],
    )
    second_rims = exchange(*out_rims)
    (result,) = call(
        functools.partial(step_kernel, False),
        [q.shape],
        [result, *second_rims, *rims, *statics, forcing],
        [pltpu.VMEM(q.shape, F32), pltpu.SemaphoreType.DMA((ROWS // 8,)), *rim_scratch],
        moved=8_000_000,
        out_hbm=True,
    )
    return result.reshape(tracers.shape), flux


def solution(mesh):
    in_specs = (
        P(None, None, "gy", "gx"),
        P(None, "gy", "gx"),
        P(None, "gy", "gx"),
        P(None, "gy", "gx"),
        P("gy", "gx"),
        P(None, "gy", "gx"),
        P("gy", "gx"),
        P("gy", "gx"),
        P("gy", "gx"),
    )
    out_specs = (P(None, None, "gy", "gx"), P(None, "gy", "gx"))
    return jax.shard_map(local, mesh=mesh, in_specs=in_specs, out_specs=out_specs, check_vma=False)
```

profile of v0, /device:TPU:57, one launch (start us, length us, event | category | flops | bytes accessed | tf_op | source)
XLA Modules:
  0.0 53.6 jit_solution(4265264025351318643)
XLA Ops:
  0.6 0.0 copy-start.3
  0.6 0.0 copy-start.4
  0.7 0.0 copy-start.5
  0.7 0.0 copy-start.8
  0.7 3.2 %shard_map.104 = (f32[64,128]{1,0:T(8,128)}, f32[64,128]{1,0:T(8,128)}, f32[384,128]{1,0:T(8,128)}, f32[384,128]{1,0:T(8,128)}, f32[224,128]{1,0:T(8,128)}, /*index=5*/f32[224,128]{1,0:T(8,128)}, f32[224,128]{1,0:T(8,128)}) custom-call(f32[16,64,256]{2,1,0:T(8,128)} %bitcast.2, f32[8,64,256]{2,1,0:T(8,128)} %east_ref.3, f32[8,64,256]{2,1,0:T(8,128)} %north_ref.3, ...), custom_call_target="tpu_custom_call" | custom-call | bytes 4000000 | tf_op jit(solution)/shard_map/pallas_call | solution.py:50
  3.9 0.8 %collective-permute-start = (f32[384,128]{1,0:T(8,128)}, f32[384,128]{1,0:T(8,128)S(1)}, u32[]{:S(2)}, u32[]{:S(2)}) collective-permute-start(f32[384,128]{1,0:T(8,128)} %get-tuple-element.18), channel_id=1, source_target_pairs={{0,1},{1,0},{2,3},{3,2},{4,5},{5,4},{6,7},{7,6},{8,9},{9,8},{10,11... | collective-permute-start | bytes 589832 | tf_op jit(solution)/shard_map/ppermute | solution.py:624
  4.6 6.8 %collective-permute-start.1 = (f32[384,128]{1,0:T(8,128)}, f32[384,128]{1,0:T(8,128)S(1)}, u32[]{:S(2)}, u32[]{:S(2)}) collective-permute-start(f32[384,128]{1,0:T(8,128)} %get-tuple-element.19), channel_id=1, source_target_pairs={{1,2},{2,1},{3,4},{4,3},{5,6},{6,5},{7,8},{8,7},{9,10},{10,9},{11,... | collective-permute-start | bytes 589832 | tf_op jit(solution)/shard_map/ppermute | solution.py:625
  11.4 1.3 %collective-permute-start.2 = (f32[224,128]{1,0:T(8,128)}, f32[224,128]{1,0:T(8,128)S(1)}, u32[]{:S(2)}, u32[]{:S(2)}) collective-permute-start(f32[224,128]{1,0:T(8,128)} %get-tuple-element.20), channel_id=1, source_target_pairs={{7,14},{8,15},{10,12},{9,11},{23,30},{24,31},{26,28},{25,27},{39,4... | collective-permute-start | bytes 344072 | tf_op jit(solution)/shard_map/ppermute | solution.py:679
  12.7 1.3 %collective-permute-start.3 = (f32[224,128]{1,0:T(8,128)}, f32[224,128]{1,0:T(8,128)S(1)}, u32[]{:S(2)}, u32[]{:S(2)}) collective-permute-start(f32[224,128]{1,0:T(8,128)} %get-tuple-element.21), channel_id=1, source_target_pairs={{8,14},{7,15},{24,30},{23,31},{40,46},{39,47},{56,62},{55,63},{72,... | collective-permute-start | bytes 344072 | tf_op jit(solution)/shard_map/ppermute | solution.py:679
  14.0 1.3 %collective-permute-start.4 = (f32[224,128]{1,0:T(8,128)}, f32[224,128]{1,0:T(8,128)S(1)}, u32[]{:S(2)}, u32[]{:S(2)}) collective-permute-start(f32[224,128]{1,0:T(8,128)} %get-tuple-element.22), channel_id=1, source_target_pairs={{9,14},{13,15},{25,30},{29,31},{41,46},{45,47},{57,62},{61,63},{73... | collective-permute-start | bytes 344072 | tf_op jit(solution)/shard_map/ppermute | solution.py:679
  15.3 0.0 collective-permute-done.refs_4_.from_sibling_ref.static_sibling_ref
  15.3 0.0 copy-done.3
  15.3 0.0 copy-done.4
  15.4 0.0 copy-done.5
  15.4 0.0 copy-done.8
  15.4 3.8 %shard_map.105.refs_4_ = f32[512,256]{1,0:T(8,128)S(1)} custom-call(s32[512,128]{1,0:T(8,128)S(1)} %copy-done.3, s32[512,128]{1,0:T(8,128)S(1)} %copy-done.4, f32[512,128]{1,0:T(8,128)S(1)} %copy-done.5, f32[8,16,128]{2,1,0:T(8,128)S(1)} %copy-done.8, f32[384,128]{1,0:T(8,128)S(1)} %collective-permute-done.refs_4_.from_sibling_ref.static_sibling_ref), custom_call_target="tpu_custom_call" | custom-call | bytes 100000 | tf_op jit(solution)/shard_map/pallas_call | solution.py:50
  19.2 0.0 copy-start.10
  19.2 0.0 copy-start.9
  19.2 0.0 collective-permute-done.2.refs_1_.refs_6_
  19.2 0.0 collective-permute-done.3.refs_2_.refs_7_
  19.3 0.8 %collective-permute-done.4.refs_3_.refs_8_ = f32[224,128]{1,0:T(8,128)S(1)} collective-permute-done((f32[224,128]{1,0:T(8,128)}, f32[224,128]{1,0:T(8,128)S(1)}, u32[]{:S(2)}, u32[]{:S(2)}) %collective-permute-start.4) | collective-permute-done | bytes 114720 | tf_op jit(solution)/shard_map/ppermute | solution.py:679
  20.1 0.0 collective-permute-done.1.refs_0_.refs_5_.from_other_ref.static_other_ref
  20.1 0.3 shard_map.106.refs_9_.more_refs_0_
  20.3 1.3 %collective-permute-start.5 = (f32[512,256]{1,0:T(8,128)S(1)}, f32[512,256]{1,0:T(8,128)S(1)}, u32[]{:S(2)}, u32[]{:S(2)}) collective-permute-start(f32[512,256]{1,0:T(8,128)S(1)} %shard_map.106.refs_9_.more_refs_0_), channel_id=1, source_target_pairs={{12,14},{11,15},{28,30},{27,31},{44,46},{43,47},{60,62},{59,63},{7... | collective-permute-start | bytes 1572872 | tf_op jit(solution)/shard_map/ppermute | solution.py:688
  21.6 0.0 copy-done.10
  21.7 0.1 collective-permute-start.6
  21.7 0.0 copy-done.9
  21.8 0.0 copy-start
  21.8 0.0 copy-start.1
  21.8 0.0 copy-start.2
  21.8 0.0 copy-start.6
  21.8 0.0 copy-start.7
  21.8 5.1 %collective-permute-start.7 = (f32[64,128]{1,0:T(8,128)S(1)}, f32[64,128]{1,0:T(8,128)S(1)}, u32[]{:S(2)}, u32[]{:S(2)}) collective-permute-start(f32[64,128]{1,0:T(8,128)S(1)} %copy-done.9), channel_id=1, source_target_pairs={{16,0},{32,16},{48,32},{64,48},{80,64},{96,80},{112,96},{0,112},{1... | collective-permute-start | bytes 98312 | tf_op jit(solution)/shard_map/ppermute | solution.py:623
  26.9 4.5 %shard_map.107.total_ref = f32[512,256]{1,0:T(8,128)S(1)} custom-call(s32[512,128]{1,0:T(8,128)S(1)} %copy-done.3, s32[512,128]{1,0:T(8,128)S(1)} %copy-done.4, f32[512,128]{1,0:T(8,128)S(1)} %copy-done.5, f32[8,16,128]{2,1,0:T(8,128)S(1)} %copy-done.8, f32[384,128]{1,0:T(8,128)S(1)} %collective-permute-done.refs_4_.from_sibling_ref.static_sibling_ref, ...), custom_call_target="tpu_custom_call" | custom-call | bytes 100000 | tf_op jit(solution)/shard_map/pallas_call | solution.py:50
  31.5 0.0 collective-permute-done.6.from_west_ref.static_west_ref
  31.5 0.0 collective-permute-done.7.from_east_ref.static_east_ref
  31.5 2.4 %shard_map.108 = (f32[16,64,256]{2,1,0:T(8,128)S(1)}, f32[8,64,256]{2,1,0:T(8,128)S(1)}) custom-call(f32[16,64,256]{2,1,0:T(8,128)S(1)} %bitcast.3, f32[64,128]{1,0:T(8,128)S(1)} %collective-permute-done.6.from_west_ref.static_west_ref, f32[64,128]{1,0:T(8,128)S(1)} %collective-permute-done.7.from_east_ref.static_east_ref, ...), custom_call_target="tpu_custom_call" | custom-call | bytes 8000000 | tf_op jit(solution)/shard_map/pallas_call | solution.py:50
  34.0 0.0 collective-permute-done.5.helped_ref
  34.0 1.3 %shard_map.109 = (f32[16,64,256]{2,1,0:T(8,128)S(1)}, f32[8,64,256]{2,1,0:T(8,128)}, f32[2,64,256]{2,1,0:T(8,128)S(1)}, f32[64,128]{1,0:T(8,128)S(1)}, f32[64,12...) custom-call(f32[512,256]{1,0:T(8,128)S(1)} %shard_map.107.total_ref, ...), custom_call_target="tpu_custom_call" | custom-call | bytes 4000000 | tf_op jit(solution)/shard_map/pallas_call | solution.py:50
  35.3 0.0 collective-permute-start.8
  35.3 5.1 %collective-permute-start.9 = (f32[64,128]{1,0:T(8,128)S(1)}, f32[64,128]{1,0:T(8,128)S(1)}, u32[]{:S(2)}, u32[]{:S(2)}) collective-permute-start(f32[64,128]{1,0:T(8,128)S(1)} %get-tuple-element.29), channel_id=1, source_target_pairs={{16,0},{32,16},{48,32},{64,48},{80,64},{96,80},{112,96},{0,112},{1... | collective-permute-start | bytes 98312 | tf_op jit(solution)/shard_map/ppermute | solution.py:623
  40.4 1.9 %collective-permute-start.10 = (f32[64,128]{1,0:T(8,128)S(1)}, f32[64,128]{1,0:T(8,128)S(1)}, u32[]{:S(2)}, u32[]{:S(2)}) collective-permute-start(f32[64,128]{1,0:T(8,128)S(1)} %get-tuple-element.30), channel_id=1, source_target_pairs={{0,1},{1,0},{2,3},{3,2},{4,5},{5,4},{6,7},{7,6},{8,9},{9,8},{10,11... | collective-permute-start | bytes 98312 | tf_op jit(solution)/shard_map/ppermute | solution.py:624
  42.2 2.1 %collective-permute-start.11 = (f32[64,128]{1,0:T(8,128)S(1)}, f32[64,128]{1,0:T(8,128)S(1)}, u32[]{:S(2)}, u32[]{:S(2)}) collective-permute-start(f32[64,128]{1,0:T(8,128)S(1)} %get-tuple-element.31), channel_id=1, source_target_pairs={{1,2},{2,1},{3,4},{4,3},{5,6},{6,5},{7,8},{8,7},{9,10},{10,9},{11,... | collective-permute-start | bytes 98312 | tf_op jit(solution)/shard_map/ppermute | solution.py:625
  44.3 0.0 collective-permute-done.8.from_west_ref
  44.4 0.0 collective-permute-done.9.from_east_ref
  44.4 0.0 collective-permute-done.10.from_sibling_ref
  44.4 6.1 %collective-permute-done.11.from_other_ref = f32[64,128]{1,0:T(8,128)S(1)} collective-permute-done((f32[64,128]{1,0:T(8,128)S(1)}, f32[64,128]{1,0:T(8,128)S(1)}, u32[]{:S(2)}, u32[]{:S(2)}) %collective-permute-start.11) | collective-permute-done | bytes 32800 | tf_op jit(solution)/shard_map/ppermute | solution.py:625
  50.5 3.1 %shard_map.110 = f32[16,64,256]{2,1,0:T(8,128)} custom-call(f32[16,64,256]{2,1,0:T(8,128)S(1)} %get-tuple-element.27.q_ref, f32[64,128]{1,0:T(8,128)S(1)} %collective-permute-done.8.from_west_ref, f32[64,128]{1,0:T(8,128)S(1)} %collective-permute-done.9.from_east_ref, f32[64,128]{1,0:T(8,128)S(1)} %collective-permute-done.10.from_sibling_ref, ...), custom_call_target="tpu_custom_call" | custom-call | bytes 8000000 | tf_op jit(solution)/shard_map/pallas_call | solution.py:50
  (5 shorter events, 0.0 us)
Async XLA Ops:
  0.6 14.7 %copy-start.3 = (s32[512,128]{1,0:T(8,128)S(1)}, s32[512,128]{1,0:T(8,128)}, u32[]{:S(2)}) copy-start(s32[512,128]{1,0:T(8,128)} %refs_0_.3) | copy-start | bytes 786436
  0.6 14.7 %copy-start.4 = (s32[512,128]{1,0:T(8,128)S(1)}, s32[512,128]{1,0:T(8,128)}, u32[]{:S(2)}) copy-start(s32[512,128]{1,0:T(8,128)} %refs_1_.5) | copy-start | bytes 786436
  0.7 14.7 %copy-start.5 = (f32[512,128]{1,0:T(8,128)S(1)}, f32[512,128]{1,0:T(8,128)}, u32[]{:S(2)}) copy-start(f32[512,128]{1,0:T(8,128)} %refs_2_.5) | copy-start | bytes 786436
  0.7 14.7 %copy-start.8 = (f32[8,16,128]{2,1,0:T(8,128)S(1)}, f32[8,16,128]{2,1,0:T(8,128)}, u32[]{:S(2)}) copy-start(f32[8,16,128]{2,1,0:T(8,128)} %refs_3_.5) | copy-start | bytes 196612
  3.9 11.5 %collective-permute-start = (f32[384,128]{1,0:T(8,128)}, f32[384,128]{1,0:T(8,128)S(1)}, u32[]{:S(2)}, u32[]{:S(2)}) collective-permute-start(f32[384,128]{1,0:T(8,128)} %get-tuple-element.18), channel_id=1, source_target_pairs={{0,1},{1,0},{2,3},{3,2},{4,5},{5,4},{6,7},{7,6},{8,9},{9,8},{10,11... | collective-permute-start | bytes 589832 | tf_op jit(solution)/shard_map/ppermute | solution.py:624
  4.6 15.4 %collective-permute-start.1 = (f32[384,128]{1,0:T(8,128)}, f32[384,128]{1,0:T(8,128)S(1)}, u32[]{:S(2)}, u32[]{:S(2)}) collective-permute-start(f32[384,128]{1,0:T(8,128)} %get-tuple-element.19), channel_id=1, source_target_pairs={{1,2},{2,1},{3,4},{4,3},{5,6},{6,5},{7,8},{8,7},{9,10},{10,9},{11,... | collective-permute-start | bytes 589832 | tf_op jit(solution)/shard_map/ppermute | solution.py:625
  11.4 7.8 %collective-permute-start.2 = (f32[224,128]{1,0:T(8,128)}, f32[224,128]{1,0:T(8,128)S(1)}, u32[]{:S(2)}, u32[]{:S(2)}) collective-permute-start(f32[224,128]{1,0:T(8,128)} %get-tuple-element.20), channel_id=1, source_target_pairs={{7,14},{8,15},{10,12},{9,11},{23,30},{24,31},{26,28},{25,27},{39,4... | collective-permute-start | bytes 344072 | tf_op jit(solution)/shard_map/ppermute | solution.py:679
  12.7 6.5 %collective-permute-start.3 = (f32[224,128]{1,0:T(8,128)}, f32[224,128]{1,0:T(8,128)S(1)}, u32[]{:S(2)}, u32[]{:S(2)}) collective-permute-start(f32[224,128]{1,0:T(8,128)} %get-tuple-element.21), channel_id=1, source_target_pairs={{8,14},{7,15},{24,30},{23,31},{40,46},{39,47},{56,62},{55,63},{72,... | collective-permute-start | bytes 344072 | tf_op jit(solution)/shard_map/ppermute | solution.py:679
  14.0 6.0 %collective-permute-start.4 = (f32[224,128]{1,0:T(8,128)}, f32[224,128]{1,0:T(8,128)S(1)}, u32[]{:S(2)}, u32[]{:S(2)}) collective-permute-start(f32[224,128]{1,0:T(8,128)} %get-tuple-element.22), channel_id=1, source_target_pairs={{9,14},{13,15},{25,30},{29,31},{41,46},{45,47},{57,62},{61,63},{73... | collective-permute-start | bytes 344072 | tf_op jit(solution)/shard_map/ppermute | solution.py:679
  19.2 2.4 %copy-start.10 = (f32[64,128]{1,0:T(8,128)S(1)}, f32[64,128]{1,0:T(8,128)}, u32[]{:S(2)}) copy-start(f32[64,128]{1,0:T(8,128)} %get-tuple-element.23) | copy-start | bytes 98308
  19.2 2.5 %copy-start.9 = (f32[64,128]{1,0:T(8,128)S(1)}, f32[64,128]{1,0:T(8,128)}, u32[]{:S(2)}) copy-start(f32[64,128]{1,0:T(8,128)} %get-tuple-element.24) | copy-start | bytes 98308
  20.3 13.6 %collective-permute-start.5 = (f32[512,256]{1,0:T(8,128)S(1)}, f32[512,256]{1,0:T(8,128)S(1)}, u32[]{:S(2)}, u32[]{:S(2)}) collective-permute-start(f32[512,256]{1,0:T(8,128)S(1)} %shard_map.106.refs_9_.more_refs_0_), channel_id=1, source_target_pairs={{12,14},{11,15},{28,30},{27,31},{44,46},{43,47},{60,62},{59,63},{7... | collective-permute-start | bytes 1572872 | tf_op jit(solution)/shard_map/ppermute | solution.py:688
  21.7 9.8 %collective-permute-start.6 = (f32[64,128]{1,0:T(8,128)S(1)}, f32[64,128]{1,0:T(8,128)S(1)}, u32[]{:S(2)}, u32[]{:S(2)}) collective-permute-start(f32[64,128]{1,0:T(8,128)S(1)} %copy-done.10), channel_id=1, source_target_pairs={{0,16},{16,32},{32,48},{48,64},{64,80},{80,96},{96,112},{112,0},{1... | collective-permute-start | bytes 98312 | tf_op jit(solution)/shard_map/ppermute | solution.py:622
  21.8 9.7 %copy-start = (f32[8,64,256]{2,1,0:T(8,128)S(1)}, f32[8,64,256]{2,1,0:T(8,128)}, u32[]{:S(2)}) copy-start(f32[8,64,256]{2,1,0:T(8,128)} %east_ref.3) | copy-start | bytes 1572868
  21.8 9.7 %copy-start.1 = (f32[8,64,256]{2,1,0:T(8,128)S(1)}, f32[8,64,256]{2,1,0:T(8,128)}, u32[]{:S(2)}) copy-start(f32[8,64,256]{2,1,0:T(8,128)} %north_ref.3) | copy-start | bytes 1572868
  21.8 9.7 %copy-start.2 = (f32[2,8,64,256]{3,2,1,0:T(8,128)S(1)}, f32[2,8,64,256]{3,2,1,0:T(8,128)}, u32[]{:S(2)}) copy-start(f32[2,8,64,256]{3,2,1,0:T(8,128)} %param.9) | copy-start | bytes 3145732
  21.8 9.7 %copy-start.6 = (f32[7,64,256]{2,1,0:T(8,128)S(1)}, f32[7,64,256]{2,1,0:T(8,128)}, u32[]{:S(2)}) copy-start(f32[7,64,256]{2,1,0:T(8,128)} %mix_ref.3) | copy-start | bytes 1376260
  21.8 9.7 %copy-start.7 = (s32[64,256]{1,0:T(8,128)S(1)}, s32[64,256]{1,0:T(8,128)}, u32[]{:S(2)}) copy-start(s32[64,256]{1,0:T(8,128)} %count_ref.3) | copy-start | bytes 196612
  21.8 9.7 %collective-permute-start.7 = (f32[64,128]{1,0:T(8,128)S(1)}, f32[64,128]{1,0:T(8,128)S(1)}, u32[]{:S(2)}, u32[]{:S(2)}) collective-permute-start(f32[64,128]{1,0:T(8,128)S(1)} %copy-done.9), channel_id=1, source_target_pairs={{16,0},{32,16},{48,32},{64,48},{80,64},{96,80},{112,96},{0,112},{1... | collective-permute-start | bytes 98312 | tf_op jit(solution)/shard_map/ppermute | solution.py:623
  35.3 9.1 %collective-permute-start.8 = (f32[64,128]{1,0:T(8,128)S(1)}, f32[64,128]{1,0:T(8,128)S(1)}, u32[]{:S(2)}, u32[]{:S(2)}) collective-permute-start(f32[64,128]{1,0:T(8,128)S(1)} %get-tuple-element.28), channel_id=1, source_target_pairs={{0,16},{16,32},{32,48},{48,64},{64,80},{80,96},{96,112},{112,0},{1... | collective-permute-start | bytes 98312 | tf_op jit(solution)/shard_map/ppermute | solution.py:622
  35.3 9.1 %collective-permute-start.9 = (f32[64,128]{1,0:T(8,128)S(1)}, f32[64,128]{1,0:T(8,128)S(1)}, u32[]{:S(2)}, u32[]{:S(2)}) collective-permute-start(f32[64,128]{1,0:T(8,128)S(1)} %get-tuple-element.29), channel_id=1, source_target_pairs={{16,0},{32,16},{48,32},{64,48},{80,64},{96,80},{112,96},{0,112},{1... | collective-permute-start | bytes 98312 | tf_op jit(solution)/shard_map/ppermute | solution.py:623
  40.4 4.0 %collective-permute-start.10 = (f32[64,128]{1,0:T(8,128)S(1)}, f32[64,128]{1,0:T(8,128)S(1)}, u32[]{:S(2)}, u32[]{:S(2)}) collective-permute-start(f32[64,128]{1,0:T(8,128)S(1)} %get-tuple-element.30), channel_id=1, source_target_pairs={{0,1},{1,0},{2,3},{3,2},{4,5},{5,4},{6,7},{7,6},{8,9},{9,8},{10,11... | collective-permute-start | bytes 98312 | tf_op jit(solution)/shard_map/ppermute | solution.py:624
  42.2 8.3 %collective-permute-start.11 = (f32[64,128]{1,0:T(8,128)S(1)}, f32[64,128]{1,0:T(8,128)S(1)}, u32[]{:S(2)}, u32[]{:S(2)}) collective-permute-start(f32[64,128]{1,0:T(8,128)S(1)} %get-tuple-element.31), channel_id=1, source_target_pairs={{1,2},{2,1},{3,4},{4,3},{5,6},{6,5},{7,8},{8,7},{9,10},{10,9},{11,... | collective-permute-start | bytes 98312 | tf_op jit(solution)/shard_map/ppermute | solution.py:625
where the time goes:
time: 54.6 us; the launch traced here: 53.6 us
  starting transfers between devices  27 us (49%)
  Pallas kernels  18.6 us (34%)
  waiting for transfers between devices  6.93 us (13%)
  between operations  0.98 us (2%)
    pallas_call x7, Pallas kernels, call(): pl.pallas_call(kernel, out_shape=[jax.ShapeDtypeStruct(shape, F32) for sh...  18.6 us
    ppermute x2, starting transfers between devices, exchange(): lax.ppermute(to_west, 'gx', WESTWARD)  10.2 us
    ppermute x2, starting transfers between devices, exchange(): lax.ppermute(other, ('gx', 'gy'), OTHERS)  8.92 us
    ppermute x2, waiting for transfers between devices, exchange(): lax.ppermute(other, ('gx', 'gy'), OTHERS)  6.09 us
    ppermute x3, starting transfers between devices, local(): lax.ppermute(part, 'gy', list(pairs))  3.88 us
    ppermute x2, starting transfers between devices, exchange(): lax.ppermute(sibling, 'gy', SIBLINGS)  2.61 us
    ppermute x1, starting transfers between devices, local(): helped = lax.ppermute(partial, 'gy', list(DENSE))  1.29 us
  transfers between devices with their start and end apart: 12, of which 2 were waited for; matrix products, arithmetic and copies ran while one was open for 0% of the time, Pallas kernels for 20%

commit v1 on v0

--- a/solution.py
+++ b/solution.py
@@ -112,7 +112,7 @@
 def pack_kernel(*refs):
     steps = len(ENTRY_STEPS)
     froms, refs = refs[:8], refs[8:]
-    (to_east_ref, to_west_ref, sibling_ref, other_ref), refs = refs[:4], refs[4:]
+    (to_east_ref, to_west_ref, sibling_ref, other_ref, fold_ref), refs = refs[:5], refs[5:]
     entry_refs, intos, (cells_ref, sems) = refs[:steps], refs[steps:-2], refs[-2:]
     tracers_ref, east_ref, north_ref, count_ref, source_ref, target_ref, weight_ref, atmos_ref = intos
     copies = [
@@ -182,6 +182,7 @@
         return count_ref[0:1, :].astype(F32)
 
     pack_rows(top_of, bottom_of, range(COUNT_AT + 1), sibling_ref, other_ref)
+    fold_ref[...] = other_ref[0 : 2 * RIM, :]
 
 
 def step_kernel(
@@ -191,10 +192,12 @@
     from_east_ref,
     from_sibling_ref,
     from_other_ref,
+    from_fold_ref,
     static_west_ref,
     static_east_ref,
     static_sibling_ref,
     static_other_ref,
+    static_fold_ref,
     east_ref,
     north_ref,
     count_ref,
@@ -213,7 +216,7 @@
     first_lane, last_lane = lane == 0, lane == LANES - 1
     first_row, last_row = row == 0, row == 7
 
-    def set_rims(sibling_rim, other_rim, south, north):
+    def set_rims(sibling_rim, other_rim, fold_rim, south, north):
         @pl.when(even)
         def _():
             south[...] = other_rim[0 : 2 * RIM, :]
@@ -229,13 +232,15 @@
             flipped = LANES - 1 - lane
             for half in range(2):
                 for block in range(RIM // 8):
-                    rows = other_rim[pl.ds((1 - half) * RIM + block * 8, 8), :]
+                    rows = fold_rim[pl.ds((1 - half) * RIM + block * 8, 8), :]
                     north[pl.ds(half * RIM + block * 8, 8), :] = jnp.take_along_axis(
                         rows, flipped, axis=1, mode="promise_in_bounds"
                     )
 
-    set_rims(from_sibling_ref, from_other_ref, from_south_ref, top_ref)
-    set_rims(static_sibling_ref, static_other_ref, static_south_ref, static_top_ref)
+    set_rims(from_sibling_ref, from_other_ref, from_fold_ref, from_south_ref, top_ref)
+    set_rims(
+        static_sibling_ref, static_other_ref, static_fold_ref, static_south_ref, static_top_ref
+    )
 
     def block_step(block, carry):
         at = pl.multiple_of(block * 8, 8)
@@ -614,15 +619,23 @@
 SIBLINGS = [(y, y ^ 1) for y in range(GY)]
 OTHERS = [
     (x * GY + y, x * GY + (y + 1 if y % 2 else y - 1)) for x in range(GX) for y in range(1, GY - 1)
-] + [(x * GY + GY - 1, (GX - 1 - x) * GY + GY - 1) for x in range(GX)]
-
-
-def exchange(to_east, to_west, sibling, other):
+]
+FOLD = [(x * GY + GY - 1, (GX - 1 - x) * GY + GY - 1) for x in range(GX)]
+
+
+def exchange(to_east, to_west, sibling, other, fold=None):
+    if fold is None:
+        others = lax.ppermute(other, ("gx", "gy"), OTHERS + FOLD)
+        folded = others
+    else:
+        others = lax.ppermute(other, ("gx", "gy"), OTHERS)
+        folded = lax.ppermute(fold, ("gx", "gy"), FOLD)
     return (
         lax.ppermute(to_east, "gx", EASTWARD),
         lax.ppermute(to_west, "gx", WESTWARD),
         lax.ppermute(sibling, "gy", SIBLINGS),
-        lax.ppermute(other, ("gx", "gy"), OTHERS),
+        others,
+        folded,
     )
 
 
@@ -666,7 +679,7 @@
     steps = len(ENTRY_STEPS)
     packed = call(
         pack_kernel,
-        [column_rim, column_rim, both, both] + [(PAYLOAD, LANES)] * steps,
+        [column_rim, column_rim, both, both, row_rim] + [(PAYLOAD, LANES)] * steps,
         [q, *statics[:3], *lists],
         [
             *[pltpu.VMEM(part.shape, part.dtype) for part in (q, *statics[:3], *lists)],
@@ -677,9 +690,9 @@
     )
     entries = [
         lax.ppermute(part, "gy", list(pairs))
-        for part, pairs in zip(packed[4:], ENTRY_STEPS, strict=True)
+        for part, pairs in zip(packed[5:], ENTRY_STEPS, strict=True)
     ]
-    rims = exchange(*packed[:4])
+    rims = exchange(*packed[:5])
     first, second, cells = 2 * RIM, 2 * RIM + LIST, 2 * RIM + 2 * LIST
     most = land([*lists, rims[2]], ((0, first, cells, None),), 1, None)
     partial = land(

time: 54.6 us -> 52.5 us (0.962); the launches traced: 53.6 us -> 52.2 us
  starting transfers between devices: 27 us -> 23.6 us
  Pallas kernels: 18.6 us -> 20.6 us
    ppermute x2 -> x3, starting transfers between devices: 8.92 us -> 5.89 us  [the longest x1 3.32 us: exchange(): folded = lax.ppermute(fold, ('gx', 'gy'), FOLD)]
    pallas_call x7, Pallas kernels: 18.6 us -> 20.6 us  [call(): pl.pallas_call(kernel, out_shape=[jax.ShapeDtypeStruct(shape, F32) for sh...]
    ppermute x2, starting transfers between devices: 10.2 us -> 8.95 us  [exchange(): lax.ppermute(to_west, 'gx', WESTWARD)]
    ppermute x2, starting transfers between devices: 0.08 us -> 1.28 us  [exchange(): lax.ppermute(to_east, 'gx', EASTWARD)]
    ppermute x2 -> x3, waiting for transfers between devices: 6.09 us -> 6.32 us  [the longest x1 6.31 us: exchange(): others = lax.ppermute(other, ('gx', 'gy'), OTHERS + FOLD)]
  transfers between devices with their start and end apart: 12 -> 13, of which waited for: 2 -> 3; matrix products, arithmetic and copies ran while one was open for 0% -> 0% of each run, Pallas kernels for 20% -> 24%
where the time goes in v1:
time: 52.5 us; the launch traced here: 52.2 us
  starting transfers between devices  23.6 us (45%)
  Pallas kernels  20.6 us (39%)
  waiting for transfers between devices  6.98 us (13%)
  between operations  0.95 us (2%)
    pallas_call x7, Pallas kernels, call(): pl.pallas_call(kernel, out_shape=[jax.ShapeDtypeStruct(shape, F32) for sh...  20.6 us
    ppermute x2, starting transfers between devices, exchange(): lax.ppermute(to_west, 'gx', WESTWARD)  8.95 us
    ppermute x1, waiting for transfers between devices, exchange(): others = lax.ppermute(other, ('gx', 'gy'), OTHERS + FOLD)  6.31 us
    ppermute x3, starting transfers between devices, local(): lax.ppermute(part, 'gy', list(pairs))  3.88 us
    ppermute x1, starting transfers between devices, exchange(): folded = lax.ppermute(fold, ('gx', 'gy'), FOLD)  3.32 us
    ppermute x2, starting transfers between devices, exchange(): lax.ppermute(sibling, 'gy', SIBLINGS)  2.34 us
    ppermute x1, starting transfers between devices, exchange(): others = lax.ppermute(other, ('gx', 'gy'), OTHERS + FOLD)  1.91 us
    ppermute x1, starting transfers between devices, local(): helped = lax.ppermute(partial, 'gy', list(DENSE))  1.29 us
  transfers between devices with their start and end apart: 13, of which 3 were waited for; matrix products, arithmetic and copies ran while one was open for 0% of the time, Pallas kernels for 24%

profile of v1, /device:TPU:57, one launch (start us, length us, event | category | flops | bytes accessed | tf_op | source)
XLA Modules:
  0.0 52.2 jit_solution(8961325162212448584)
XLA Ops:
  0.6 0.0 copy-start.3
  0.6 0.0 copy-start.4
  0.7 0.0 copy-start.5
  0.7 0.0 copy-start.8
  0.7 3.2 %shard_map.104 = (f32[64,128]{1,0:T(8,128)}, f32[64,128]{1,0:T(8,128)}, f32[384,128]{1,0:T(8,128)}, f32[384,128]{1,0:T(8,128)}, f32[64,128]{1,0:T(8,128)}, /*ind...) custom-call(f32[16,64,256]{2,1,0:T(8,128)} %bitcast.2, f32[8,64,256]{2,1,0:T(8,128)} %east_ref.3, ...), custom_call_target="tpu_custom_call" | custom-call | bytes 4000000 | tf_op jit(solution)/shard_map/pallas_call | solution.py:50
  3.9 0.8 %collective-permute-start = (f32[384,128]{1,0:T(8,128)}, f32[384,128]{1,0:T(8,128)S(1)}, u32[]{:S(2)}, u32[]{:S(2)}) collective-permute-start(f32[384,128]{1,0:T(8,128)} %get-tuple-element.19), channel_id=1, source_target_pairs={{0,1},{1,0},{2,3},{3,2},{4,5},{5,4},{6,7},{7,6},{8,9},{9,8},{10,11... | collective-permute-start | bytes 589832 | tf_op jit(solution)/shard_map/ppermute | solution.py:636
  4.7 0.7 %collective-permute-start.1 = (f32[384,128]{1,0:T(8,128)}, f32[384,128]{1,0:T(8,128)S(1)}, u32[]{:S(2)}, u32[]{:S(2)}) collective-permute-start(f32[384,128]{1,0:T(8,128)} %get-tuple-element.20), channel_id=1, source_target_pairs={{1,2},{2,1},{3,4},{4,3},{5,6},{6,5},{7,8},{8,7},{9,10},{10,9},{11,... | collective-permute-start | bytes 589832 | tf_op jit(solution)/shard_map/ppermute | solution.py:631
  5.3 1.3 %collective-permute-start.2 = (f32[224,128]{1,0:T(8,128)}, f32[224,128]{1,0:T(8,128)S(1)}, u32[]{:S(2)}, u32[]{:S(2)}) collective-permute-start(f32[224,128]{1,0:T(8,128)} %get-tuple-element.21), channel_id=1, source_target_pairs={{7,14},{8,15},{10,12},{9,11},{23,30},{24,31},{26,28},{25,27},{39,4... | collective-permute-start | bytes 344072 | tf_op jit(solution)/shard_map/ppermute | solution.py:692
  6.6 1.3 %collective-permute-start.3 = (f32[224,128]{1,0:T(8,128)}, f32[224,128]{1,0:T(8,128)S(1)}, u32[]{:S(2)}, u32[]{:S(2)}) collective-permute-start(f32[224,128]{1,0:T(8,128)} %get-tuple-element.22), channel_id=1, source_target_pairs={{8,14},{7,15},{24,30},{23,31},{40,46},{39,47},{56,62},{55,63},{72,... | collective-permute-start | bytes 344072 | tf_op jit(solution)/shard_map/ppermute | solution.py:692
  7.9 1.3 %collective-permute-start.4 = (f32[224,128]{1,0:T(8,128)}, f32[224,128]{1,0:T(8,128)S(1)}, u32[]{:S(2)}, u32[]{:S(2)}) collective-permute-start(f32[224,128]{1,0:T(8,128)} %get-tuple-element.23), channel_id=1, source_target_pairs={{9,14},{13,15},{25,30},{29,31},{41,46},{45,47},{57,62},{61,63},{73... | collective-permute-start | bytes 344072 | tf_op jit(solution)/shard_map/ppermute | solution.py:692
  9.2 0.0 collective-permute-done.refs_4_.from_sibling_ref.static_sibling_ref
  9.2 0.0 copy-done.3
  9.3 0.0 copy-done.4
  9.3 0.0 copy-done.5
  9.3 0.0 copy-done.8
  9.3 4.4 %shard_map.105.refs_4_ = f32[512,256]{1,0:T(8,128)S(1)} custom-call(s32[512,128]{1,0:T(8,128)S(1)} %copy-done.3, s32[512,128]{1,0:T(8,128)S(1)} %copy-done.4, f32[512,128]{1,0:T(8,128)S(1)} %copy-done.5, f32[8,16,128]{2,1,0:T(8,128)S(1)} %copy-done.8, f32[384,128]{1,0:T(8,128)S(1)} %collective-permute-done.refs_4_.from_sibling_ref.static_sibling_ref), custom_call_target="tpu_custom_call" | custom-call | bytes 100000 | tf_op jit(solution)/shard_map/pallas_call | solution.py:50
  13.7 0.0 copy-start.11
  13.7 0.0 copy-start.10
  13.7 0.0 copy-start.9
  13.7 0.1 collective-permute-done.2.refs_1_.refs_6_
  13.8 0.5 %collective-permute-done.3.refs_2_.refs_7_ = f32[224,128]{1,0:T(8,128)S(1)} collective-permute-done((f32[224,128]{1,0:T(8,128)}, f32[224,128]{1,0:T(8,128)S(1)}, u32[]{:S(2)}, u32[]{:S(2)}) %collective-permute-start.3) | collective-permute-done | bytes 114720 | tf_op jit(solution)/shard_map/ppermute | solution.py:692
  14.4 0.0 collective-permute-done.4.refs_3_.refs_8_
  14.4 0.0 collective-permute-done.1.refs_0_.refs_5_.from_other_ref.static_other_ref
  14.4 0.3 shard_map.106.refs_9_.more_refs_0_
  14.7 1.3 %collective-permute-start.5 = (f32[512,256]{1,0:T(8,128)S(1)}, f32[512,256]{1,0:T(8,128)S(1)}, u32[]{:S(2)}, u32[]{:S(2)}) collective-permute-start(f32[512,256]{1,0:T(8,128)S(1)} %shard_map.106.refs_9_.more_refs_0_), channel_id=1, source_target_pairs={{12,14},{11,15},{28,30},{27,31},{44,46},{43,47},{60,62},{59,63},{7... | collective-permute-start | bytes 1572872 | tf_op jit(solution)/shard_map/ppermute | solution.py:701
  16.0 0.0 copy-done.11
  16.0 1.3 %collective-permute-start.6 = (f32[64,128]{1,0:T(8,128)S(1)}, f32[64,128]{1,0:T(8,128)S(1)}, u32[]{:S(2)}, u32[]{:S(2)}) collective-permute-start(f32[64,128]{1,0:T(8,128)S(1)} %copy-done.11), channel_id=1, source_target_pairs={{0,16},{16,32},{32,48},{48,64},{64,80},{80,96},{96,112},{112,0},{1... | collective-permute-start | bytes 98312 | tf_op jit(solution)/shard_map/ppermute | solution.py:634
  17.2 0.0 copy-done.10
  17.2 3.9 %collective-permute-start.7 = (f32[64,128]{1,0:T(8,128)S(1)}, f32[64,128]{1,0:T(8,128)S(1)}, u32[]{:S(2)}, u32[]{:S(2)}) collective-permute-start(f32[64,128]{1,0:T(8,128)S(1)} %copy-done.10), channel_id=1, source_target_pairs={{16,0},{32,16},{48,32},{64,48},{80,64},{96,80},{112,96},{0,112},{1... | collective-permute-start | bytes 98312 | tf_op jit(solution)/shard_map/ppermute | solution.py:635
  21.1 0.0 copy-start.6
  21.1 0.0 copy-start.7
  21.1 3.3 %collective-permute-start.8 = (f32[64,128]{1,0:T(8,128)S(1)}, f32[64,128]{1,0:T(8,128)S(1)}, u32[]{:S(2)}, u32[]{:S(2)}) collective-permute-start(f32[64,128]{1,0:T(8,128)S(1)} %copy-done.9), channel_id=1, source_target_pairs={{15,127},{31,111},{47,95},{63,79},{79,63},{95,47},{111,31},{127,15}} | collective-permute-start | bytes 98312 | tf_op jit(solution)/shard_map/ppermute | solution.py:632
  24.5 5.9 %shard_map.107.total_ref = f32[512,256]{1,0:T(8,128)S(1)} custom-call(s32[512,128]{1,0:T(8,128)S(1)} %copy-done.3, s32[512,128]{1,0:T(8,128)S(1)} %copy-done.4, f32[512,128]{1,0:T(8,128)S(1)} %copy-done.5, f32[8,16,128]{2,1,0:T(8,128)S(1)} %copy-done.8, f32[384,128]{1,0:T(8,128)S(1)} %collective-permute-done.refs_4_.from_sibling_ref.static_sibling_ref, ...), custom_call_target="tpu_custom_call" | custom-call | bytes 100000 | tf_op jit(solution)/shard_map/pallas_call | solution.py:50
  30.4 0.0 collective-permute-done.6.from_west_ref.static_west_ref
  30.4 0.0 collective-permute-done.7.from_east_ref.static_east_ref
  30.4 0.0 collective-permute-done.8.from_fold_ref.static_fold_ref
  30.5 2.4 %shard_map.108 = (f32[16,64,256]{2,1,0:T(8,128)S(1)}, f32[8,64,256]{2,1,0:T(8,128)S(1)}) custom-call(f32[16,64,256]{2,1,0:T(8,128)S(1)} %bitcast.3, f32[64,128]{1,0:T(8,128)S(1)} %collective-permute-done.6.from_west_ref.static_west_ref, f32[64,128]{1,0:T(8,128)S(1)} %collective-permute-done.7.from_east_ref.static_east_ref, ...), custom_call_target="tpu_custom_call" | custom-call | bytes 8000000 | tf_op jit(solution)/shard_map/pallas_call | solution.py:50
  32.9 0.0 collective-permute-done.5.helped_ref
  32.9 1.3 %shard_map.109 = (f32[16,64,256]{2,1,0:T(8,128)S(1)}, f32[8,64,256]{2,1,0:T(8,128)}, f32[2,64,256]{2,1,0:T(8,128)S(1)}, f32[64,128]{1,0:T(8,128)S(1)}, f32[64,12...) custom-call(f32[512,256]{1,0:T(8,128)S(1)} %shard_map.107.total_ref, ...), custom_call_target="tpu_custom_call" | custom-call | bytes 4000000 | tf_op jit(solution)/shard_map/pallas_call | solution.py:50
  34.2 0.0 collective-permute-start.9
  34.2 5.1 %collective-permute-start.10 = (f32[64,128]{1,0:T(8,128)S(1)}, f32[64,128]{1,0:T(8,128)S(1)}, u32[]{:S(2)}, u32[]{:S(2)}) collective-permute-start(f32[64,128]{1,0:T(8,128)S(1)} %get-tuple-element.31), channel_id=1, source_target_pairs={{16,0},{32,16},{48,32},{64,48},{80,64},{96,80},{112,96},{0,112},{1... | collective-permute-start | bytes 98312 | tf_op jit(solution)/shard_map/ppermute | solution.py:635
  39.3 1.6 %collective-permute-start.11 = (f32[64,128]{1,0:T(8,128)S(1)}, f32[64,128]{1,0:T(8,128)S(1)}, u32[]{:S(2)}, u32[]{:S(2)}) collective-permute-start(f32[64,128]{1,0:T(8,128)S(1)} %get-tuple-element.32), channel_id=1, source_target_pairs={{0,1},{1,0},{2,3},{3,2},{4,5},{5,4},{6,7},{7,6},{8,9},{9,8},{10,11... | collective-permute-start | bytes 98312 | tf_op jit(solution)/shard_map/ppermute | solution.py:636
  40.9 1.9 %collective-permute-start.12 = (f32[64,128]{1,0:T(8,128)S(1)}, f32[64,128]{1,0:T(8,128)S(1)}, u32[]{:S(2)}, u32[]{:S(2)}) collective-permute-start(f32[64,128]{1,0:T(8,128)S(1)} %get-tuple-element.33), channel_id=1, source_target_pairs={{1,2},{2,1},{3,4},{4,3},{5,6},{6,5},{7,8},{8,7},{9,10},{10,9},{11,... | collective-permute-start | bytes 98312 | tf_op jit(solution)/shard_map/ppermute | solution.py:628
  42.8 0.0 collective-permute-done.9.from_west_ref
  42.8 0.0 collective-permute-done.10.from_east_ref
  42.8 0.0 collective-permute-done.11.from_sibling_ref
  42.8 6.3 %collective-permute-done.12.from_other_ref.from_fold_ref = f32[64,128]{1,0:T(8,128)S(1)} collective-permute-done((f32[64,128]{1,0:T(8,128)S(1)}, f32[64,128]{1,0:T(8,128)S(1)}, u32[]{:S(2)}, u32[]{:S(2)}) %collective-permute-start.12) | collective-permute-done | bytes 32800 | tf_op jit(solution)/shard_map/ppermute | solution.py:628
  49.1 3.1 %shard_map.110 = f32[16,64,256]{2,1,0:T(8,128)} custom-call(f32[16,64,256]{2,1,0:T(8,128)S(1)} %get-tuple-element.29.q_ref, f32[64,128]{1,0:T(8,128)S(1)} %collective-permute-done.9.from_west_ref, f32[64,128]{1,0:T(8,128)S(1)} %collective-permute-done.10.from_east_ref, f32[64,128]{1,0:T(8,128)S(1)} %collective-permute-done.11.from_sibling_ref, ...), custom_call_target="tpu_custom_call" | custom-call | bytes 8000000 | tf_op jit(solution)/shard_map/pallas_call | solution.py:50
  (9 shorter events, 0.0 us)
Async XLA Ops:
  0.6 8.6 %copy-start.3 = (s32[512,128]{1,0:T(8,128)S(1)}, s32[512,128]{1,0:T(8,128)}, u32[]{:S(2)}) copy-start(s32[512,128]{1,0:T(8,128)} %refs_0_.3) | copy-start | bytes 786436
  0.6 8.6 %copy-start.4 = (s32[512,128]{1,0:T(8,128)S(1)}, s32[512,128]{1,0:T(8,128)}, u32[]{:S(2)}) copy-start(s32[512,128]{1,0:T(8,128)} %refs_1_.5) | copy-start | bytes 786436
  0.7 8.6 %copy-start.5 = (f32[512,128]{1,0:T(8,128)S(1)}, f32[512,128]{1,0:T(8,128)}, u32[]{:S(2)}) copy-start(f32[512,128]{1,0:T(8,128)} %refs_2_.5) | copy-start | bytes 786436
  0.7 8.6 %copy-start.8 = (f32[8,16,128]{2,1,0:T(8,128)S(1)}, f32[8,16,128]{2,1,0:T(8,128)}, u32[]{:S(2)}) copy-start(f32[8,16,128]{2,1,0:T(8,128)} %refs_3_.5) | copy-start | bytes 196612
  3.9 5.3 %collective-permute-start = (f32[384,128]{1,0:T(8,128)}, f32[384,128]{1,0:T(8,128)S(1)}, u32[]{:S(2)}, u32[]{:S(2)}) collective-permute-start(f32[384,128]{1,0:T(8,128)} %get-tuple-element.19), channel_id=1, source_target_pairs={{0,1},{1,0},{2,3},{3,2},{4,5},{5,4},{6,7},{7,6},{8,9},{9,8},{10,11... | collective-permute-start | bytes 589832 | tf_op jit(solution)/shard_map/ppermute | solution.py:636
  4.7 9.7 %collective-permute-start.1 = (f32[384,128]{1,0:T(8,128)}, f32[384,128]{1,0:T(8,128)S(1)}, u32[]{:S(2)}, u32[]{:S(2)}) collective-permute-start(f32[384,128]{1,0:T(8,128)} %get-tuple-element.20), channel_id=1, source_target_pairs={{1,2},{2,1},{3,4},{4,3},{5,6},{6,5},{7,8},{8,7},{9,10},{10,9},{11,... | collective-permute-start | bytes 589832 | tf_op jit(solution)/shard_map/ppermute | solution.py:631
  5.3 8.5 %collective-permute-start.2 = (f32[224,128]{1,0:T(8,128)}, f32[224,128]{1,0:T(8,128)S(1)}, u32[]{:S(2)}, u32[]{:S(2)}) collective-permute-start(f32[224,128]{1,0:T(8,128)} %get-tuple-element.21), channel_id=1, source_target_pairs={{7,14},{8,15},{10,12},{9,11},{23,30},{24,31},{26,28},{25,27},{39,4... | collective-permute-start | bytes 344072 | tf_op jit(solution)/shard_map/ppermute | solution.py:692
  6.6 7.7 %collective-permute-start.3 = (f32[224,128]{1,0:T(8,128)}, f32[224,128]{1,0:T(8,128)S(1)}, u32[]{:S(2)}, u32[]{:S(2)}) collective-permute-start(f32[224,128]{1,0:T(8,128)} %get-tuple-element.22), channel_id=1, source_target_pairs={{8,14},{7,15},{24,30},{23,31},{40,46},{39,47},{56,62},{55,63},{72,... | collective-permute-start | bytes 344072 | tf_op jit(solution)/shard_map/ppermute | solution.py:692
  7.9 6.4 %collective-permute-start.4 = (f32[224,128]{1,0:T(8,128)}, f32[224,128]{1,0:T(8,128)S(1)}, u32[]{:S(2)}, u32[]{:S(2)}) collective-permute-start(f32[224,128]{1,0:T(8,128)} %get-tuple-element.23), channel_id=1, source_target_pairs={{9,14},{13,15},{25,30},{29,31},{41,46},{45,47},{57,62},{61,63},{73... | collective-permute-start | bytes 344072 | tf_op jit(solution)/shard_map/ppermute | solution.py:692
  13.7 2.3 %copy-start.11 = (f32[64,128]{1,0:T(8,128)S(1)}, f32[64,128]{1,0:T(8,128)}, u32[]{:S(2)}) copy-start(f32[64,128]{1,0:T(8,128)} %get-tuple-element.24) | copy-start | bytes 98308
  13.7 3.5 %copy-start.10 = (f32[64,128]{1,0:T(8,128)S(1)}, f32[64,128]{1,0:T(8,128)}, u32[]{:S(2)}) copy-start(f32[64,128]{1,0:T(8,128)} %get-tuple-element.25) | copy-start | bytes 98308
  13.7 7.4 %copy-start.9 = (f32[64,128]{1,0:T(8,128)S(1)}, f32[64,128]{1,0:T(8,128)}, u32[]{:S(2)}) copy-start(f32[64,128]{1,0:T(8,128)} %get-tuple-element.26) | copy-start | bytes 98308
  14.7 18.2 %collective-permute-start.5 = (f32[512,256]{1,0:T(8,128)S(1)}, f32[512,256]{1,0:T(8,128)S(1)}, u32[]{:S(2)}, u32[]{:S(2)}) collective-permute-start(f32[512,256]{1,0:T(8,128)S(1)} %shard_map.106.refs_9_.more_refs_0_), channel_id=1, source_target_pairs={{12,14},{11,15},{28,30},{27,31},{44,46},{43,47},{60,62},{59,63},{7... | collective-permute-start | bytes 1572872 | tf_op jit(solution)/shard_map/ppermute | solution.py:701
  16.0 14.4 %collective-permute-start.6 = (f32[64,128]{1,0:T(8,128)S(1)}, f32[64,128]{1,0:T(8,128)S(1)}, u32[]{:S(2)}, u32[]{:S(2)}) collective-permute-start(f32[64,128]{1,0:T(8,128)S(1)} %copy-done.11), channel_id=1, source_target_pairs={{0,16},{16,32},{32,48},{48,64},{64,80},{80,96},{96,112},{112,0},{1... | collective-permute-start | bytes 98312 | tf_op jit(solution)/shard_map/ppermute | solution.py:634
  17.2 13.2 %collective-permute-start.7 = (f32[64,128]{1,0:T(8,128)S(1)}, f32[64,128]{1,0:T(8,128)S(1)}, u32[]{:S(2)}, u32[]{:S(2)}) collective-permute-start(f32[64,128]{1,0:T(8,128)S(1)} %copy-done.10), channel_id=1, source_target_pairs={{16,0},{32,16},{48,32},{64,48},{80,64},{96,80},{112,96},{0,112},{1... | collective-permute-start | bytes 98312 | tf_op jit(solution)/shard_map/ppermute | solution.py:635
  21.1 9.3 %copy-start = (f32[8,64,256]{2,1,0:T(8,128)S(1)}, f32[8,64,256]{2,1,0:T(8,128)}, u32[]{:S(2)}) copy-start(f32[8,64,256]{2,1,0:T(8,128)} %east_ref.3) | copy-start | bytes 1572868
  21.1 9.3 %copy-start.1 = (f32[8,64,256]{2,1,0:T(8,128)S(1)}, f32[8,64,256]{2,1,0:T(8,128)}, u32[]{:S(2)}) copy-start(f32[8,64,256]{2,1,0:T(8,128)} %north_ref.3) | copy-start | bytes 1572868
  21.1 9.3 %copy-start.2 = (f32[2,8,64,256]{3,2,1,0:T(8,128)S(1)}, f32[2,8,64,256]{3,2,1,0:T(8,128)}, u32[]{:S(2)}) copy-start(f32[2,8,64,256]{3,2,1,0:T(8,128)} %param.9) | copy-start | bytes 3145732
  21.1 9.3 %copy-start.6 = (f32[7,64,256]{2,1,0:T(8,128)S(1)}, f32[7,64,256]{2,1,0:T(8,128)}, u32[]{:S(2)}) copy-start(f32[7,64,256]{2,1,0:T(8,128)} %mix_ref.3) | copy-start | bytes 1376260
  21.1 9.3 %copy-start.7 = (s32[64,256]{1,0:T(8,128)S(1)}, s32[64,256]{1,0:T(8,128)}, u32[]{:S(2)}) copy-start(s32[64,256]{1,0:T(8,128)} %count_ref.3) | copy-start | bytes 196612
  21.1 9.3 %collective-permute-start.8 = (f32[64,128]{1,0:T(8,128)S(1)}, f32[64,128]{1,0:T(8,128)S(1)}, u32[]{:S(2)}, u32[]{:S(2)}) collective-permute-start(f32[64,128]{1,0:T(8,128)S(1)} %copy-done.9), channel_id=1, source_target_pairs={{15,127},{31,111},{47,95},{63,79},{79,63},{95,47},{111,31},{127,15}} | collective-permute-start | bytes 98312 | tf_op jit(solution)/shard_map/ppermute | solution.py:632
  34.2 8.6 %collective-permute-start.9 = (f32[64,128]{1,0:T(8,128)S(1)}, f32[64,128]{1,0:T(8,128)S(1)}, u32[]{:S(2)}, u32[]{:S(2)}) collective-permute-start(f32[64,128]{1,0:T(8,128)S(1)} %get-tuple-element.30), channel_id=1, source_target_pairs={{0,16},{16,32},{32,48},{48,64},{64,80},{80,96},{96,112},{112,0},{1... | collective-permute-start | bytes 98312 | tf_op jit(solution)/shard_map/ppermute | solution.py:634
  34.2 8.6 %collective-permute-start.10 = (f32[64,128]{1,0:T(8,128)S(1)}, f32[64,128]{1,0:T(8,128)S(1)}, u32[]{:S(2)}, u32[]{:S(2)}) collective-permute-start(f32[64,128]{1,0:T(8,128)S(1)} %get-tuple-element.31), channel_id=1, source_target_pairs={{16,0},{32,16},{48,32},{64,48},{80,64},{96,80},{112,96},{0,112},{1... | collective-permute-start | bytes 98312 | tf_op jit(solution)/shard_map/ppermute | solution.py:635
  39.3 3.5 %collective-permute-start.11 = (f32[64,128]{1,0:T(8,128)S(1)}, f32[64,128]{1,0:T(8,128)S(1)}, u32[]{:S(2)}, u32[]{:S(2)}) collective-permute-start(f32[64,128]{1,0:T(8,128)S(1)} %get-tuple-element.32), channel_id=1, source_target_pairs={{0,1},{1,0},{2,3},{3,2},{4,5},{5,4},{6,7},{7,6},{8,9},{9,8},{10,11... | collective-permute-start | bytes 98312 | tf_op jit(solution)/shard_map/ppermute | solution.py:636
  40.9 8.3 %collective-permute-start.12 = (f32[64,128]{1,0:T(8,128)S(1)}, f32[64,128]{1,0:T(8,128)S(1)}, u32[]{:S(2)}, u32[]{:S(2)}) collective-permute-start(f32[64,128]{1,0:T(8,128)S(1)} %get-tuple-element.33), channel_id=1, source_target_pairs={{1,2},{2,1},{3,4},{4,3},{5,6},{6,5},{7,8},{8,7},{9,10},{10,9},{11,... | collective-permute-start | bytes 98312 | tf_op jit(solution)/shard_map/ppermute | solution.py:628

commit v2 on v1

--- a/solution.py
+++ b/solution.py
@@ -58,16 +58,26 @@
     )(*operands)
 
 
-def pack_columns(pick, channels, out_ref):
+def is_odd_column():
+    return lax.rem(lax.axis_index("gx"), 2) == 1
+
+
+def pack_columns(east_of, east_channels, west_of, west_channels, far_ref, near_ref):
+    odd = is_odd_column()
     lane = lax.broadcasted_iota(jnp.int32, (8, LANES), 1)
     for block in range(ROWS // 8):
-        tile = jnp.zeros((8, LANES), F32)
-        for channel in channels:
-            value, at = pick(channel, block * 8)
-            shift = (channel - at) % LANES
-            moved = pltpu.roll(value, shift, axis=1) if shift else value
-            tile = jnp.where(lane == channel, moved, tile)
-        out_ref[pl.ds(block * 8, 8), :] = tile
+        tiles = []
+        for pick, channels in ((east_of, east_channels), (west_of, west_channels)):
+            tile = jnp.zeros((8, LANES), F32)
+            for channel in channels:
+                value, at = pick(channel, block * 8)
+                shift = (channel - at) % LANES
+                moved = pltpu.roll(value, shift, axis=1) if shift else value
+                tile = jnp.where(lane == channel, moved, tile)
+            tiles.append(tile)
+        east, west = tiles
+        far_ref[pl.ds(block * 8, 8), :] = jnp.where(odd, east, west)
+        near_ref[pl.ds(block * 8, 8), :] = jnp.where(odd, west, east)
 
 
 def pack_row(value, channel, out_ref):
@@ -112,7 +122,7 @@
 def pack_kernel(*refs):
     steps = len(ENTRY_STEPS)
     froms, refs = refs[:8], refs[8:]
-    (to_east_ref, to_west_ref, sibling_ref, other_ref, fold_ref), refs = refs[:5], refs[5:]
+    (to_far_ref, to_near_ref, sibling_ref, other_ref, fold_ref), refs = refs[:5], refs[5:]
     entry_refs, intos, (cells_ref, sems) = refs[:steps], refs[steps:-2], refs[-2:]
     tracers_ref, east_ref, north_ref, count_ref, source_ref, target_ref, weight_ref, atmos_ref = intos
     copies = [
@@ -164,8 +174,14 @@
             return tracers_ref[channel, rows, :LANES], 0
         return count_ref[rows, :LANES].astype(F32), 0
 
-    pack_columns(east_column, [*range(CHANNELS + NZ), COUNT_AT], to_east_ref)
-    pack_columns(west_column, [*range(CHANNELS), COUNT_AT], to_west_ref)
+    pack_columns(
+        east_column,
+        [*range(CHANNELS + NZ), COUNT_AT],
+        west_column,
+        [*range(CHANNELS), COUNT_AT],
+        to_far_ref,
+        to_near_ref,
+    )
 
     def top_of(channel):
         if channel < CHANNELS:
@@ -188,13 +204,13 @@
 def step_kernel(
     forced,
     q_ref,
-    from_west_ref,
-    from_east_ref,
+    from_far_ref,
+    from_near_ref,
     from_sibling_ref,
     from_other_ref,
     from_fold_ref,
-    static_west_ref,
-    static_east_ref,
+    static_far_ref,
+    static_near_ref,
     static_sibling_ref,
     static_other_ref,
     static_fold_ref,
@@ -205,10 +221,16 @@
     *more_refs,
 ):
     if forced:
-        out_ref, gain_ref = more_refs[-6:-4]
+        out_ref, gain_ref = more_refs[-10:-8]
     else:
         forcing_ref, out_hbm, out_ref, sems = more_refs[:4]
-    from_south_ref, top_ref, static_south_ref, static_top_ref = more_refs[-4:]
+    from_south_ref, top_ref, static_south_ref, static_top_ref = more_refs[-8:-4]
+    from_west_ref, from_east_ref, static_west_ref, static_east_ref = more_refs[-4:]
+    odd = is_odd_column()
+    from_west_ref[...] = jnp.where(odd, from_near_ref[...], from_far_ref[...])
+    from_east_ref[...] = jnp.where(odd, from_far_ref[...], from_near_ref[...])
+    static_west_ref[...] = jnp.where(odd, static_near_ref[...], static_far_ref[...])
+    static_east_ref[...] = jnp.where(odd, static_far_ref[...], static_near_ref[...])
     even = is_even()
     on_top = lax.axis_index("gy") == GY - 1
     lane = lax.broadcasted_iota(jnp.int32, (8, LANES), 1)
@@ -570,8 +592,8 @@
     result_ref,
     flux_ref,
     forcing_ref,
-    to_east_ref,
-    to_west_ref,
+    to_far_ref,
+    to_near_ref,
     sibling_ref,
     other_ref,
 ):
@@ -598,12 +620,10 @@
     pack_columns(
         lambda channel, row: (result_ref[channel, pl.ds(row, 8), LANES:], LANES - 1),
         range(CHANNELS),
-        to_east_ref,
-    )
-    pack_columns(
         lambda channel, row: (result_ref[channel, pl.ds(row, 8), :LANES], 0),
         range(CHANNELS),
-        to_west_ref,
+        to_far_ref,
+        to_near_ref,
     )
     pack_rows(
         lambda channel: result_ref[channel, ROWS - 1 : ROWS, :],
@@ -614,8 +634,8 @@
     )
 
 
-EASTWARD = [(i, (i + 1) % GX) for i in range(GX)]
-WESTWARD = [((i + 1) % GX, i) for i in range(GX)]
+FAR = [(x, (x + 1 if x % 2 else x - 1) % GX) for x in range(GX)]
+NEAR = [(x, (x - 1 if x % 2 else x + 1) % GX) for x in range(GX)]
 SIBLINGS = [(y, y ^ 1) for y in range(GY)]
 OTHERS = [
     (x * GY + y, x * GY + (y + 1 if y % 2 else y - 1)) for x in range(GX) for y in range(1, GY - 1)
@@ -623,7 +643,7 @@
 FOLD = [(x * GY + GY - 1, (GX - 1 - x) * GY + GY - 1) for x in range(GX)]
 
 
-def exchange(to_east, to_west, sibling, other, fold=None):
+def exchange(to_far, to_near, sibling, other, fold=None):
     if fold is None:
         others = lax.ppermute(other, ("gx", "gy"), OTHERS + FOLD)
         folded = others
@@ -631,8 +651,8 @@
         others = lax.ppermute(other, ("gx", "gy"), OTHERS)
         folded = lax.ppermute(fold, ("gx", "gy"), FOLD)
     return (
-        lax.ppermute(to_east, "gx", EASTWARD),
-        lax.ppermute(to_west, "gx", WESTWARD),
+        lax.ppermute(to_far, "gx", FAR),
+        lax.ppermute(to_near, "gx", NEAR),
         lax.ppermute(sibling, "gy", SIBLINGS),
         others,
         folded,
@@ -706,7 +726,7 @@
         1,
         True,
     )
-    rim_scratch = [pltpu.VMEM(row_rim, F32)] * 4
+    rim_scratch = [pltpu.VMEM(row_rim, F32)] * 4 + [pltpu.VMEM(column_rim, F32)] * 4
     solved, gain = call(
         functools.partial(step_kernel, True),
         [q.shape, east_speed.shape],

time: 52.5 us -> 50.5 us (0.962)
  waiting for transfers between devices: 6.98 us -> 5.14 us
    ppermute x1, starting transfers between devices: 1.91 us -> 3.96 us  [exchange(): others = lax.ppermute(other, ('gx', 'gy'), OTHERS + FOLD)]
    ppermute x1, waiting for transfers between devices: 6.31 us -> 4.26 us  [exchange(): others = lax.ppermute(other, ('gx', 'gy'), OTHERS + FOLD)]
    ppermute x2, starting transfers between devices: 2.34 us -> 0.76 us  [exchange(): lax.ppermute(sibling, 'gy', SIBLINGS)]
    pallas_call x7, Pallas kernels: 20.6 us -> 20.1 us  [call(): pl.pallas_call(kernel, out_shape=[jax.ShapeDtypeStruct(shape, F32) for sh...]
  transfers between devices with their start and end apart: 13 -> 13, of which waited for: 3 -> 4; matrix products, arithmetic and copies ran while one was open for 0% -> 0% of each run, Pallas kernels for 24% -> 24%
where the time goes in v2:
time: 50.5 us; the launch traced here: 50 us
  starting transfers between devices  23.8 us (47%)
  Pallas kernels  20.1 us (40%)
  waiting for transfers between devices  5.14 us (10%)
  between operations  0.95 us (2%)
    pallas_call x7, Pallas kernels, call(): pl.pallas_call(kernel, out_shape=[jax.ShapeDtypeStruct(shape, F32) for sh...  20.1 us
    ppermute x2, starting transfers between devices, exchange(): lax.ppermute(to_far, 'gx', FAR)  10.5 us
    ppermute x1, waiting for transfers between devices, exchange(): others = lax.ppermute(other, ('gx', 'gy'), OTHERS + FOLD)  4.26 us
    ppermute x1, starting transfers between devices, exchange(): others = lax.ppermute(other, ('gx', 'gy'), OTHERS + FOLD)  3.96 us
    ppermute x3, starting transfers between devices, local(): lax.ppermute(part, 'gy', list(pairs))  3.88 us
    ppermute x1, starting transfers between devices, exchange(): folded = lax.ppermute(fold, ('gx', 'gy'), FOLD)  2.81 us
    ppermute x1, starting transfers between devices, local(): helped = lax.ppermute(partial, 'gy', list(DENSE))  1.29 us
  transfers between devices with their start and end apart: 13, of which 4 were waited for; matrix products, arithmetic and copies ran while one was open for 0% of the time, Pallas kernels for 24%

profile of v2, /device:TPU:57, one launch (start us, length us, event | category | flops | bytes accessed | tf_op | source)
XLA Modules:
  0.0 50.0 jit_solution(777997362414840408)
XLA Ops:
  0.6 0.0 copy-start.3
  0.6 0.0 copy-start.4
  0.7 0.0 copy-start.5
  0.7 0.0 copy-start.8
  0.7 3.2 %shard_map.104 = (f32[64,128]{1,0:T(8,128)}, f32[64,128]{1,0:T(8,128)}, f32[384,128]{1,0:T(8,128)}, f32[384,128]{1,0:T(8,128)}, f32[64,128]{1,0:T(8,128)}, /*ind...) custom-call(f32[16,64,256]{2,1,0:T(8,128)} %bitcast.2, f32[8,64,256]{2,1,0:T(8,128)} %east_ref.3, ...), custom_call_target="tpu_custom_call" | custom-call | bytes 4000000 | tf_op jit(solution)/shard_map/pallas_call | solution.py:50
  3.9 0.8 %collective-permute-start = (f32[384,128]{1,0:T(8,128)}, f32[384,128]{1,0:T(8,128)S(1)}, u32[]{:S(2)}, u32[]{:S(2)}) collective-permute-start(f32[384,128]{1,0:T(8,128)} %get-tuple-element.19), channel_id=1, source_target_pairs={{0,1},{1,0},{2,3},{3,2},{4,5},{5,4},{6,7},{7,6},{8,9},{9,8},{10,11... | collective-permute-start | bytes 589832 | tf_op jit(solution)/shard_map/ppermute | solution.py:656
  4.6 0.7 %collective-permute-start.1 = (f32[384,128]{1,0:T(8,128)}, f32[384,128]{1,0:T(8,128)S(1)}, u32[]{:S(2)}, u32[]{:S(2)}) collective-permute-start(f32[384,128]{1,0:T(8,128)} %get-tuple-element.20), channel_id=1, source_target_pairs={{1,2},{2,1},{3,4},{4,3},{5,6},{6,5},{7,8},{8,7},{9,10},{10,9},{11,... | collective-permute-start | bytes 589832 | tf_op jit(solution)/shard_map/ppermute | solution.py:651
  5.3 1.3 %collective-permute-start.2 = (f32[224,128]{1,0:T(8,128)}, f32[224,128]{1,0:T(8,128)S(1)}, u32[]{:S(2)}, u32[]{:S(2)}) collective-permute-start(f32[224,128]{1,0:T(8,128)} %get-tuple-element.21), channel_id=1, source_target_pairs={{7,14},{8,15},{10,12},{9,11},{23,30},{24,31},{26,28},{25,27},{39,4... | collective-permute-start | bytes 344072 | tf_op jit(solution)/shard_map/ppermute | solution.py:712
  6.6 1.3 %collective-permute-start.3 = (f32[224,128]{1,0:T(8,128)}, f32[224,128]{1,0:T(8,128)S(1)}, u32[]{:S(2)}, u32[]{:S(2)}) collective-permute-start(f32[224,128]{1,0:T(8,128)} %get-tuple-element.22), channel_id=1, source_target_pairs={{8,14},{7,15},{24,30},{23,31},{40,46},{39,47},{56,62},{55,63},{72,... | collective-permute-start | bytes 344072 | tf_op jit(solution)/shard_map/ppermute | solution.py:712
  7.9 1.3 %collective-permute-start.4 = (f32[224,128]{1,0:T(8,128)}, f32[224,128]{1,0:T(8,128)S(1)}, u32[]{:S(2)}, u32[]{:S(2)}) collective-permute-start(f32[224,128]{1,0:T(8,128)} %get-tuple-element.23), channel_id=1, source_target_pairs={{9,14},{13,15},{25,30},{29,31},{41,46},{45,47},{57,62},{61,63},{73... | collective-permute-start | bytes 344072 | tf_op jit(solution)/shard_map/ppermute | solution.py:712
  9.2 0.0 collective-permute-done.refs_4_.from_sibling_ref.static_sibling_ref
  9.2 0.0 copy-done.3
  9.2 0.0 copy-done.4
  9.3 4.4 %shard_map.105.refs_4_ = f32[512,256]{1,0:T(8,128)S(1)} custom-call(s32[512,128]{1,0:T(8,128)S(1)} %copy-done.3, s32[512,128]{1,0:T(8,128)S(1)} %copy-done.4, f32[512,128]{1,0:T(8,128)S(1)} %copy-done.5, f32[8,16,128]{2,1,0:T(8,128)S(1)} %copy-done.8, f32[384,128]{1,0:T(8,128)S(1)} %collective-permute-done.refs_4_.from_sibling_ref.static_sibling_ref), custom_call_target="tpu_custom_call" | custom-call | bytes 100000 | tf_op jit(solution)/shard_map/pallas_call | solution.py:50
  13.7 0.1 collective-permute-done.2.refs_1_.refs_6_
  13.8 0.5 %collective-permute-done.3.refs_2_.refs_7_ = f32[224,128]{1,0:T(8,128)S(1)} collective-permute-done((f32[224,128]{1,0:T(8,128)}, f32[224,128]{1,0:T(8,128)S(1)}, u32[]{:S(2)}, u32[]{:S(2)}) %collective-permute-start.3) | collective-permute-done | bytes 114720 | tf_op jit(solution)/shard_map/ppermute | solution.py:712
  14.3 0.0 collective-permute-done.4.refs_3_.refs_8_
  14.3 0.0 collective-permute-done.1.refs_0_.refs_5_.from_other_ref.static_other_ref
  14.3 0.3 shard_map.106.refs_9_.more_refs_0_
  14.6 1.3 %collective-permute-start.5 = (f32[512,256]{1,0:T(8,128)S(1)}, f32[512,256]{1,0:T(8,128)S(1)}, u32[]{:S(2)}, u32[]{:S(2)}) collective-permute-start(f32[512,256]{1,0:T(8,128)S(1)} %shard_map.106.refs_9_.more_refs_0_), channel_id=1, source_target_pairs={{12,14},{11,15},{28,30},{27,31},{44,46},{43,47},{60,62},{59,63},{7... | collective-permute-start | bytes 1572872 | tf_op jit(solution)/shard_map/ppermute | solution.py:721
  15.9 5.0 %collective-permute-start.6 = (f32[64,128]{1,0:T(8,128)S(1)}, f32[64,128]{1,0:T(8,128)S(1)}, u32[]{:S(2)}, u32[]{:S(2)}) collective-permute-start(f32[64,128]{1,0:T(8,128)S(1)} %copy-done.11), channel_id=1, source_target_pairs={{0,112},{16,32},{32,16},{48,64},{64,48},{80,96},{96,80},{112,0},{1... | collective-permute-start | bytes 98312 | tf_op jit(solution)/shard_map/ppermute | solution.py:654
  20.9 0.0 copy-done.10
  20.9 0.0 collective-permute-start.7
  20.9 0.0 copy-start
  20.9 0.0 copy-start.1
  20.9 0.0 copy-start.2
  21.0 0.0 copy-start.6
  21.0 0.0 copy-start.7
  21.0 2.8 %collective-permute-start.8 = (f32[64,128]{1,0:T(8,128)S(1)}, f32[64,128]{1,0:T(8,128)S(1)}, u32[]{:S(2)}, u32[]{:S(2)}) collective-permute-start(f32[64,128]{1,0:T(8,128)S(1)} %copy-done.9), channel_id=1, source_target_pairs={{15,127},{31,111},{47,95},{63,79},{79,63},{95,47},{111,31},{127,15}} | collective-permute-start | bytes 98312 | tf_op jit(solution)/shard_map/ppermute | solution.py:652
  23.8 5.3 %shard_map.107.total_ref = f32[512,256]{1,0:T(8,128)S(1)} custom-call(s32[512,128]{1,0:T(8,128)S(1)} %copy-done.3, s32[512,128]{1,0:T(8,128)S(1)} %copy-done.4, f32[512,128]{1,0:T(8,128)S(1)} %copy-done.5, f32[8,16,128]{2,1,0:T(8,128)S(1)} %copy-done.8, f32[384,128]{1,0:T(8,128)S(1)} %collective-permute-done.refs_4_.from_sibling_ref.static_sibling_ref, ...), custom_call_target="tpu_custom_call" | custom-call | bytes 100000 | tf_op jit(solution)/shard_map/pallas_call | solution.py:50
  29.2 0.0 collective-permute-done.6.from_far_ref.static_far_ref
  29.2 0.0 collective-permute-done.7.from_near_ref.static_near_ref
  29.2 0.2 collective-permute-done.8.from_fold_ref.static_fold_ref
  29.4 0.0 copy-done.2
  29.4 0.0 copy-done.6
  29.4 0.0 copy-done.7
  29.4 2.4 %shard_map.108 = (f32[16,64,256]{2,1,0:T(8,128)S(1)}, f32[8,64,256]{2,1,0:T(8,128)S(1)}) custom-call(f32[16,64,256]{2,1,0:T(8,128)S(1)} %bitcast.3, f32[64,128]{1,0:T(8,128)S(1)} %collective-permute-done.6.from_far_ref.static_far_ref, f32[64,128]{1,0:T(8,128)S(1)} %collective-permute-done.7.from_near_ref.static_near_ref, ...), custom_call_target="tpu_custom_call" | custom-call | bytes 8000000 | tf_op jit(solution)/shard_map/pallas_call | solution.py:50
  31.9 0.0 collective-permute-done.5.helped_ref
  31.9 1.3 %shard_map.109 = (f32[16,64,256]{2,1,0:T(8,128)S(1)}, f32[8,64,256]{2,1,0:T(8,128)}, f32[2,64,256]{2,1,0:T(8,128)S(1)}, f32[64,128]{1,0:T(8,128)S(1)}, f32[64,12...) custom-call(f32[512,256]{1,0:T(8,128)S(1)} %shard_map.107.total_ref, ...), custom_call_target="tpu_custom_call" | custom-call | bytes 4000000 | tf_op jit(solution)/shard_map/pallas_call | solution.py:50
  33.2 5.5 %collective-permute-start.9 = (f32[64,128]{1,0:T(8,128)S(1)}, f32[64,128]{1,0:T(8,128)S(1)}, u32[]{:S(2)}, u32[]{:S(2)}) collective-permute-start(f32[64,128]{1,0:T(8,128)S(1)} %get-tuple-element.30), channel_id=1, source_target_pairs={{0,112},{16,32},{32,16},{48,64},{64,48},{80,96},{96,80},{112,0},{1... | collective-permute-start | bytes 98312 | tf_op jit(solution)/shard_map/ppermute | solution.py:654
  38.7 0.0 collective-permute-start.10
  38.7 0.0 collective-permute-start.11
  38.7 4.0 %collective-permute-start.12 = (f32[64,128]{1,0:T(8,128)S(1)}, f32[64,128]{1,0:T(8,128)S(1)}, u32[]{:S(2)}, u32[]{:S(2)}) collective-permute-start(f32[64,128]{1,0:T(8,128)S(1)} %get-tuple-element.33), channel_id=1, source_target_pairs={{1,2},{2,1},{3,4},{4,3},{5,6},{6,5},{7,8},{8,7},{9,10},{10,9},{11,... | collective-permute-start | bytes 98312 | tf_op jit(solution)/shard_map/ppermute | solution.py:648
  42.6 0.0 collective-permute-done.9.from_far_ref
  42.7 0.0 collective-permute-done.10.from_near_ref
  42.7 0.0 collective-permute-done.11.from_sibling_ref
  42.7 4.3 %collective-permute-done.12.from_other_ref.from_fold_ref = f32[64,128]{1,0:T(8,128)S(1)} collective-permute-done((f32[64,128]{1,0:T(8,128)S(1)}, f32[64,128]{1,0:T(8,128)S(1)}, u32[]{:S(2)}, u32[]{:S(2)}) %collective-permute-start.12) | collective-permute-done | bytes 32800 | tf_op jit(solution)/shard_map/ppermute | solution.py:648
  46.9 3.1 %shard_map.110 = f32[16,64,256]{2,1,0:T(8,128)} custom-call(f32[16,64,256]{2,1,0:T(8,128)S(1)} %get-tuple-element.29.q_ref, f32[64,128]{1,0:T(8,128)S(1)} %collective-permute-done.9.from_far_ref, f32[64,128]{1,0:T(8,128)S(1)} %collective-permute-done.10.from_near_ref, f32[64,128]{1,0:T(8,128)S(1)} %collective-permute-done.11.from_sibling_ref, ...), custom_call_target="tpu_custom_call" | custom-call | bytes 8000000 | tf_op jit(solution)/shard_map/pallas_call | solution.py:50
  (9 shorter events, 0.0 us)
Async XLA Ops:
  0.6 8.6 %copy-start.3 = (s32[512,128]{1,0:T(8,128)S(1)}, s32[512,128]{1,0:T(8,128)}, u32[]{:S(2)}) copy-start(s32[512,128]{1,0:T(8,128)} %refs_0_.3) | copy-start | bytes 786436
  0.6 8.6 %copy-start.4 = (s32[512,128]{1,0:T(8,128)S(1)}, s32[512,128]{1,0:T(8,128)}, u32[]{:S(2)}) copy-start(s32[512,128]{1,0:T(8,128)} %refs_1_.5) | copy-start | bytes 786436
  0.7 8.6 %copy-start.5 = (f32[512,128]{1,0:T(8,128)S(1)}, f32[512,128]{1,0:T(8,128)}, u32[]{:S(2)}) copy-start(f32[512,128]{1,0:T(8,128)} %refs_2_.5) | copy-start | bytes 786436
  0.7 8.6 %copy-start.8 = (f32[8,16,128]{2,1,0:T(8,128)S(1)}, f32[8,16,128]{2,1,0:T(8,128)}, u32[]{:S(2)}) copy-start(f32[8,16,128]{2,1,0:T(8,128)} %refs_3_.5) | copy-start | bytes 196612
  3.9 5.3 %collective-permute-start = (f32[384,128]{1,0:T(8,128)}, f32[384,128]{1,0:T(8,128)S(1)}, u32[]{:S(2)}, u32[]{:S(2)}) collective-permute-start(f32[384,128]{1,0:T(8,128)} %get-tuple-element.19), channel_id=1, source_target_pairs={{0,1},{1,0},{2,3},{3,2},{4,5},{5,4},{6,7},{7,6},{8,9},{9,8},{10,11... | collective-permute-start | bytes 589832 | tf_op jit(solution)/shard_map/ppermute | solution.py:656
  4.6 9.7 %collective-permute-start.1 = (f32[384,128]{1,0:T(8,128)}, f32[384,128]{1,0:T(8,128)S(1)}, u32[]{:S(2)}, u32[]{:S(2)}) collective-permute-start(f32[384,128]{1,0:T(8,128)} %get-tuple-element.20), channel_id=1, source_target_pairs={{1,2},{2,1},{3,4},{4,3},{5,6},{6,5},{7,8},{8,7},{9,10},{10,9},{11,... | collective-permute-start | bytes 589832 | tf_op jit(solution)/shard_map/ppermute | solution.py:651
  5.3 8.5 %collective-permute-start.2 = (f32[224,128]{1,0:T(8,128)}, f32[224,128]{1,0:T(8,128)S(1)}, u32[]{:S(2)}, u32[]{:S(2)}) collective-permute-start(f32[224,128]{1,0:T(8,128)} %get-tuple-element.21), channel_id=1, source_target_pairs={{7,14},{8,15},{10,12},{9,11},{23,30},{24,31},{26,28},{25,27},{39,4... | collective-permute-start | bytes 344072 | tf_op jit(solution)/shard_map/ppermute | solution.py:712
  6.6 7.7 %collective-permute-start.3 = (f32[224,128]{1,0:T(8,128)}, f32[224,128]{1,0:T(8,128)S(1)}, u32[]{:S(2)}, u32[]{:S(2)}) collective-permute-start(f32[224,128]{1,0:T(8,128)} %get-tuple-element.22), channel_id=1, source_target_pairs={{8,14},{7,15},{24,30},{23,31},{40,46},{39,47},{56,62},{55,63},{72,... | collective-permute-start | bytes 344072 | tf_op jit(solution)/shard_map/ppermute | solution.py:712
  7.9 6.4 %collective-permute-start.4 = (f32[224,128]{1,0:T(8,128)}, f32[224,128]{1,0:T(8,128)S(1)}, u32[]{:S(2)}, u32[]{:S(2)}) collective-permute-start(f32[224,128]{1,0:T(8,128)} %get-tuple-element.23), channel_id=1, source_target_pairs={{9,14},{13,15},{25,30},{29,31},{41,46},{45,47},{57,62},{61,63},{73... | collective-permute-start | bytes 344072 | tf_op jit(solution)/shard_map/ppermute | solution.py:712
  13.7 2.3 %copy-start.11 = (f32[64,128]{1,0:T(8,128)S(1)}, f32[64,128]{1,0:T(8,128)}, u32[]{:S(2)}) copy-start(f32[64,128]{1,0:T(8,128)} %get-tuple-element.24) | copy-start | bytes 98308
  13.7 7.2 %copy-start.10 = (f32[64,128]{1,0:T(8,128)S(1)}, f32[64,128]{1,0:T(8,128)}, u32[]{:S(2)}) copy-start(f32[64,128]{1,0:T(8,128)} %get-tuple-element.25) | copy-start | bytes 98308
  13.7 7.2 %copy-start.9 = (f32[64,128]{1,0:T(8,128)S(1)}, f32[64,128]{1,0:T(8,128)}, u32[]{:S(2)}) copy-start(f32[64,128]{1,0:T(8,128)} %get-tuple-element.26) | copy-start | bytes 98308
  14.6 17.2 %collective-permute-start.5 = (f32[512,256]{1,0:T(8,128)S(1)}, f32[512,256]{1,0:T(8,128)S(1)}, u32[]{:S(2)}, u32[]{:S(2)}) collective-permute-start(f32[512,256]{1,0:T(8,128)S(1)} %shard_map.106.refs_9_.more_refs_0_), channel_id=1, source_target_pairs={{12,14},{11,15},{28,30},{27,31},{44,46},{43,47},{60,62},{59,63},{7... | collective-permute-start | bytes 1572872 | tf_op jit(solution)/shard_map/ppermute | solution.py:721
  15.9 13.2 %collective-permute-start.6 = (f32[64,128]{1,0:T(8,128)S(1)}, f32[64,128]{1,0:T(8,128)S(1)}, u32[]{:S(2)}, u32[]{:S(2)}) collective-permute-start(f32[64,128]{1,0:T(8,128)S(1)} %copy-done.11), channel_id=1, source_target_pairs={{0,112},{16,32},{32,16},{48,64},{64,48},{80,96},{96,80},{112,0},{1... | collective-permute-start | bytes 98312 | tf_op jit(solution)/shard_map/ppermute | solution.py:654
  20.9 8.3 %collective-permute-start.7 = (f32[64,128]{1,0:T(8,128)S(1)}, f32[64,128]{1,0:T(8,128)S(1)}, u32[]{:S(2)}, u32[]{:S(2)}) collective-permute-start(f32[64,128]{1,0:T(8,128)S(1)} %copy-done.10), channel_id=1, source_target_pairs={{0,16},{16,0},{32,48},{48,32},{64,80},{80,64},{96,112},{112,96},{1... | collective-permute-start | bytes 98312 | tf_op jit(solution)/shard_map/ppermute | solution.py:655
  20.9 8.5 %copy-start = (f32[8,64,256]{2,1,0:T(8,128)S(1)}, f32[8,64,256]{2,1,0:T(8,128)}, u32[]{:S(2)}) copy-start(f32[8,64,256]{2,1,0:T(8,128)} %east_ref.3) | copy-start | bytes 1572868
  20.9 8.5 %copy-start.1 = (f32[8,64,256]{2,1,0:T(8,128)S(1)}, f32[8,64,256]{2,1,0:T(8,128)}, u32[]{:S(2)}) copy-start(f32[8,64,256]{2,1,0:T(8,128)} %north_ref.3) | copy-start | bytes 1572868
  20.9 8.4 %copy-start.2 = (f32[2,8,64,256]{3,2,1,0:T(8,128)S(1)}, f32[2,8,64,256]{3,2,1,0:T(8,128)}, u32[]{:S(2)}) copy-start(f32[2,8,64,256]{3,2,1,0:T(8,128)} %param.9) | copy-start | bytes 3145732
  21.0 8.4 %copy-start.6 = (f32[7,64,256]{2,1,0:T(8,128)S(1)}, f32[7,64,256]{2,1,0:T(8,128)}, u32[]{:S(2)}) copy-start(f32[7,64,256]{2,1,0:T(8,128)} %mix_ref.3) | copy-start | bytes 1376260
  21.0 8.4 %copy-start.7 = (s32[64,256]{1,0:T(8,128)S(1)}, s32[64,256]{1,0:T(8,128)}, u32[]{:S(2)}) copy-start(s32[64,256]{1,0:T(8,128)} %count_ref.3) | copy-start | bytes 196612
  21.0 8.4 %collective-permute-start.8 = (f32[64,128]{1,0:T(8,128)S(1)}, f32[64,128]{1,0:T(8,128)S(1)}, u32[]{:S(2)}, u32[]{:S(2)}) collective-permute-start(f32[64,128]{1,0:T(8,128)S(1)} %copy-done.9), channel_id=1, source_target_pairs={{15,127},{31,111},{47,95},{63,79},{79,63},{95,47},{111,31},{127,15}} | collective-permute-start | bytes 98312 | tf_op jit(solution)/shard_map/ppermute | solution.py:652
  33.2 9.5 %collective-permute-start.9 = (f32[64,128]{1,0:T(8,128)S(1)}, f32[64,128]{1,0:T(8,128)S(1)}, u32[]{:S(2)}, u32[]{:S(2)}) collective-permute-start(f32[64,128]{1,0:T(8,128)S(1)} %get-tuple-element.30), channel_id=1, source_target_pairs={{0,112},{16,32},{32,16},{48,64},{64,48},{80,96},{96,80},{112,0},{1... | collective-permute-start | bytes 98312 | tf_op jit(solution)/shard_map/ppermute | solution.py:654
  38.7 4.0 %collective-permute-start.10 = (f32[64,128]{1,0:T(8,128)S(1)}, f32[64,128]{1,0:T(8,128)S(1)}, u32[]{:S(2)}, u32[]{:S(2)}) collective-permute-start(f32[64,128]{1,0:T(8,128)S(1)} %get-tuple-element.31), channel_id=1, source_target_pairs={{0,16},{16,0},{32,48},{48,32},{64,80},{80,64},{96,112},{112,96},{1... | collective-permute-start | bytes 98312 | tf_op jit(solution)/shard_map/ppermute | solution.py:655
  38.7 4.0 %collective-permute-start.11 = (f32[64,128]{1,0:T(8,128)S(1)}, f32[64,128]{1,0:T(8,128)S(1)}, u32[]{:S(2)}, u32[]{:S(2)}) collective-permute-start(f32[64,128]{1,0:T(8,128)S(1)} %get-tuple-element.32), channel_id=1, source_target_pairs={{0,1},{1,0},{2,3},{3,2},{4,5},{5,4},{6,7},{7,6},{8,9},{9,8},{10,11... | collective-permute-start | bytes 98312 | tf_op jit(solution)/shard_map/ppermute | solution.py:656
  38.7 8.3 %collective-permute-start.12 = (f32[64,128]{1,0:T(8,128)S(1)}, f32[64,128]{1,0:T(8,128)S(1)}, u32[]{:S(2)}, u32[]{:S(2)}) collective-permute-start(f32[64,128]{1,0:T(8,128)S(1)} %get-tuple-element.33), channel_id=1, source_target_pairs={{1,2},{2,1},{3,4},{4,3},{5,6},{6,5},{7,8},{8,7},{9,10},{10,9},{11,... | collective-permute-start | bytes 98312 | tf_op jit(solution)/shard_map/ppermute | solution.py:648

commit v3 on v2

--- a/solution.py
+++ b/solution.py
@@ -649,7 +649,7 @@
         folded = others
     else:
         others = lax.ppermute(other, ("gx", "gy"), OTHERS)
-        folded = lax.ppermute(fold, ("gx", "gy"), FOLD)
+        folded = fold
     return (
         lax.ppermute(to_far, "gx", FAR),
         lax.ppermute(to_near, "gx", NEAR),
@@ -726,6 +726,8 @@
         1,
         True,
     )
+    fold, _ = lax.optimization_barrier((rims[4], total))
+    rims = (*rims[:4], lax.ppermute(fold, ("gx", "gy"), FOLD))
     rim_scratch = [pltpu.VMEM(row_rim, F32)] * 4 + [pltpu.VMEM(column_rim, F32)] * 4
     solved, gain = call(
         functools.partial(step_kernel, True),

time: 50.5 us -> 51.2 us (1.014)
  waiting for transfers between devices: 5.14 us -> 8.82 us
  starting transfers between devices: 23.8 us -> 21.9 us
  Pallas kernels: 20.1 us -> 19.5 us
    ppermute x1, waiting for transfers between devices: 0.21 us -> 4.98 us  [local(): rims = (*rims[:4], lax.ppermute(fold, ('gx', 'gy'), FOLD))]
    ppermute x2, starting transfers between devices: 10.5 us -> 6.33 us  [exchange(): lax.ppermute(to_far, 'gx', FAR)]
    ppermute x1, waiting for transfers between devices: 4.26 us -> 2.6 us  [exchange(): others = lax.ppermute(other, ('gx', 'gy'), OTHERS + FOLD)]
    ppermute x1, starting transfers between devices: 3.96 us -> 5.62 us  [exchange(): others = lax.ppermute(other, ('gx', 'gy'), OTHERS + FOLD)]
    ppermute x3, waiting for transfers between devices: 0.64 us -> 1.22 us  [local(): lax.ppermute(part, 'gy', list(pairs))]
    pallas_call x7, Pallas kernels: 20.1 us -> 19.5 us  [call(): pl.pallas_call(kernel, out_shape=[jax.ShapeDtypeStruct(shape, F32) for sh...]
  transfers between devices with their start and end apart: 13 -> 13, of which waited for: 4 -> 4; matrix products, arithmetic and copies ran while one was open for 0% -> 0% of each run, Pallas kernels for 24% -> 23%
where the time goes in v3:
time: 51.2 us
  starting transfers between devices  21.9 us (43%)
  Pallas kernels  19.5 us (38%)
  waiting for transfers between devices  8.82 us (17%)
  between operations  0.93 us (2%)
    pallas_call x7, Pallas kernels, call(): pl.pallas_call(kernel, out_shape=[jax.ShapeDtypeStruct(shape, F32) for sh...  19.5 us
    ppermute x2, starting transfers between devices, exchange(): lax.ppermute(to_far, 'gx', FAR)  6.33 us
    ppermute x1, starting transfers between devices, exchange(): others = lax.ppermute(other, ('gx', 'gy'), OTHERS + FOLD)  5.62 us
    ppermute x1, waiting for transfers between devices, local(): rims = (*rims[:4], lax.ppermute(fold, ('gx', 'gy'), FOLD))  4.98 us
    ppermute x3, starting transfers between devices, local(): lax.ppermute(part, 'gy', list(pairs))  3.88 us
    ppermute x1, starting transfers between devices, local(): rims = (*rims[:4], lax.ppermute(fold, ('gx', 'gy'), FOLD))  3.27 us
    ppermute x1, waiting for transfers between devices, exchange(): others = lax.ppermute(other, ('gx', 'gy'), OTHERS + FOLD)  2.6 us
    ppermute x1, starting transfers between devices, local(): helped = lax.ppermute(partial, 'gy', list(DENSE))  1.29 us
  transfers between devices with their start and end apart: 13, of which 4 were waited for; matrix products, arithmetic and copies ran while one was open for 0% of the time, Pallas kernels for 23%

profile of v3, /device:TPU:57, one launch (start us, length us, event | category | flops | bytes accessed | tf_op | source)
XLA Modules:
  0.0 51.2 jit_solution(5269846422180553650)
XLA Ops:
  0.6 0.0 copy-start.3
  0.6 0.0 copy-start.4
  0.7 0.0 copy-start.5
  0.7 0.0 copy-start.8
  0.7 3.2 %shard_map.104 = (f32[64,128]{1,0:T(8,128)}, f32[64,128]{1,0:T(8,128)}, f32[384,128]{1,0:T(8,128)}, f32[384,128]{1,0:T(8,128)}, f32[64,128]{1,0:T(8,128)}, /*ind...) custom-call(f32[16,64,256]{2,1,0:T(8,128)} %bitcast.2, f32[8,64,256]{2,1,0:T(8,128)} %east_ref.3, ...), custom_call_target="tpu_custom_call" | custom-call | bytes 4000000 | tf_op jit(solution)/shard_map/pallas_call | solution.py:50
  3.9 0.8 %collective-permute-start = (f32[384,128]{1,0:T(8,128)}, f32[384,128]{1,0:T(8,128)S(1)}, u32[]{:S(2)}, u32[]{:S(2)}) collective-permute-start(f32[384,128]{1,0:T(8,128)} %get-tuple-element.20), channel_id=1, source_target_pairs={{0,1},{1,0},{2,3},{3,2},{4,5},{5,4},{6,7},{7,6},{8,9},{9,8},{10,11... | collective-permute-start | bytes 589832 | tf_op jit(solution)/shard_map/ppermute | solution.py:656
  4.6 0.7 %collective-permute-start.1 = (f32[384,128]{1,0:T(8,128)}, f32[384,128]{1,0:T(8,128)S(1)}, u32[]{:S(2)}, u32[]{:S(2)}) collective-permute-start(f32[384,128]{1,0:T(8,128)} %get-tuple-element.21), channel_id=1, source_target_pairs={{1,2},{2,1},{3,4},{4,3},{5,6},{6,5},{7,8},{8,7},{9,10},{10,9},{11,... | collective-permute-start | bytes 589832 | tf_op jit(solution)/shard_map/ppermute | solution.py:651
  5.3 1.3 %collective-permute-start.2 = (f32[224,128]{1,0:T(8,128)}, f32[224,128]{1,0:T(8,128)S(1)}, u32[]{:S(2)}, u32[]{:S(2)}) collective-permute-start(f32[224,128]{1,0:T(8,128)} %get-tuple-element.22), channel_id=1, source_target_pairs={{7,14},{8,15},{10,12},{9,11},{23,30},{24,31},{26,28},{25,27},{39,4... | collective-permute-start | bytes 344072 | tf_op jit(solution)/shard_map/ppermute | solution.py:712
  6.6 1.3 %collective-permute-start.3 = (f32[224,128]{1,0:T(8,128)}, f32[224,128]{1,0:T(8,128)S(1)}, u32[]{:S(2)}, u32[]{:S(2)}) collective-permute-start(f32[224,128]{1,0:T(8,128)} %get-tuple-element.23), channel_id=1, source_target_pairs={{8,14},{7,15},{24,30},{23,31},{40,46},{39,47},{56,62},{55,63},{72,... | collective-permute-start | bytes 344072 | tf_op jit(solution)/shard_map/ppermute | solution.py:712
  7.9 1.3 %collective-permute-start.4 = (f32[224,128]{1,0:T(8,128)}, f32[224,128]{1,0:T(8,128)S(1)}, u32[]{:S(2)}, u32[]{:S(2)}) collective-permute-start(f32[224,128]{1,0:T(8,128)} %get-tuple-element.24), channel_id=1, source_target_pairs={{9,14},{13,15},{25,30},{29,31},{41,46},{45,47},{57,62},{61,63},{73... | collective-permute-start | bytes 344072 | tf_op jit(solution)/shard_map/ppermute | solution.py:712
  9.2 0.0 collective-permute-done.refs_4_.from_sibling_ref.static_sibling_ref
  9.2 0.0 copy-done.3
  9.2 0.0 copy-done.4
  9.2 0.0 copy-done.5
  9.3 0.0 copy-done.8
  9.3 3.8 %shard_map.105.refs_4_ = f32[512,256]{1,0:T(8,128)S(1)} custom-call(s32[512,128]{1,0:T(8,128)S(1)} %copy-done.3, s32[512,128]{1,0:T(8,128)S(1)} %copy-done.4, f32[512,128]{1,0:T(8,128)S(1)} %copy-done.5, f32[8,16,128]{2,1,0:T(8,128)S(1)} %copy-done.8, f32[384,128]{1,0:T(8,128)S(1)} %collective-permute-done.refs_4_.from_sibling_ref.static_sibling_ref), custom_call_target="tpu_custom_call" | custom-call | bytes 100000 | tf_op jit(solution)/shard_map/pallas_call | solution.py:50
  13.1 0.0 copy-start.11
  13.1 0.0 copy-start.10
  13.1 0.7 %collective-permute-done.2.refs_1_.refs_6_ = f32[224,128]{1,0:T(8,128)S(1)} collective-permute-done((f32[224,128]{1,0:T(8,128)}, f32[224,128]{1,0:T(8,128)S(1)}, u32[]{:S(2)}, u32[]{:S(2)}) %collective-permute-start.2) | collective-permute-done | bytes 114720 | tf_op jit(solution)/shard_map/ppermute | solution.py:712
  13.8 0.5 %collective-permute-done.3.refs_2_.refs_7_ = f32[224,128]{1,0:T(8,128)S(1)} collective-permute-done((f32[224,128]{1,0:T(8,128)}, f32[224,128]{1,0:T(8,128)S(1)}, u32[]{:S(2)}, u32[]{:S(2)}) %collective-permute-start.3) | collective-permute-done | bytes 114720 | tf_op jit(solution)/shard_map/ppermute | solution.py:712
  14.3 0.0 collective-permute-done.4.refs_3_.refs_8_
  14.3 0.0 collective-permute-done.1.refs_0_.refs_5_.from_other_ref.static_other_ref
  14.4 0.3 shard_map.106.refs_9_.more_refs_0_
  14.6 1.3 %collective-permute-start.5 = (f32[512,256]{1,0:T(8,128)S(1)}, f32[512,256]{1,0:T(8,128)S(1)}, u32[]{:S(2)}, u32[]{:S(2)}) collective-permute-start(f32[512,256]{1,0:T(8,128)S(1)} %shard_map.106.refs_9_.more_refs_0_), channel_id=1, source_target_pairs={{12,14},{11,15},{28,30},{27,31},{44,46},{43,47},{60,62},{59,63},{7... | collective-permute-start | bytes 1572872 | tf_op jit(solution)/shard_map/ppermute | solution.py:721
  15.9 0.0 copy-done.11
  15.9 5.0 %collective-permute-start.6 = (f32[64,128]{1,0:T(8,128)S(1)}, f32[64,128]{1,0:T(8,128)S(1)}, u32[]{:S(2)}, u32[]{:S(2)}) collective-permute-start(f32[64,128]{1,0:T(8,128)S(1)} %copy-done.11), channel_id=1, source_target_pairs={{0,112},{16,32},{32,16},{48,64},{64,48},{80,96},{96,80},{112,0},{1... | collective-permute-start | bytes 98312 | tf_op jit(solution)/shard_map/ppermute | solution.py:654
  20.9 0.0 copy-done.10
  20.9 0.0 copy-start.6
  20.9 0.0 copy-start.7
  21.0 0.1 collective-permute-start.7
  21.0 5.3 %shard_map.107.total_ref = f32[512,256]{1,0:T(8,128)S(1)} custom-call(s32[512,128]{1,0:T(8,128)S(1)} %copy-done.3, s32[512,128]{1,0:T(8,128)S(1)} %copy-done.4, f32[512,128]{1,0:T(8,128)S(1)} %copy-done.5, f32[8,16,128]{2,1,0:T(8,128)S(1)} %copy-done.8, f32[384,128]{1,0:T(8,128)S(1)} %collective-permute-done.refs_4_.from_sibling_ref.static_sibling_ref, ...), custom_call_target="tpu_custom_call" | custom-call | bytes 100000 | tf_op jit(solution)/shard_map/pallas_call | solution.py:50
  26.4 3.3 %collective-permute-start.8 = (f32[64,128]{1,0:T(8,128)S(1)}, f32[64,128]{1,0:T(8,128)S(1)}, u32[]{:S(2)}, u32[]{:S(2)}) collective-permute-start(f32[64,128]{1,0:T(8,128)S(1)} %copy-done.9), channel_id=1, source_target_pairs={{15,127},{31,111},{47,95},{63,79},{79,63},{95,47},{111,31},{127,15}} | collective-permute-start | bytes 98312 | tf_op jit(solution)/shard_map/ppermute | solution.py:730
  29.7 0.0 collective-permute-done.6.from_far_ref.static_far_ref
  29.7 0.0 collective-permute-done.7.from_near_ref.static_near_ref
  29.7 5.0 %collective-permute-done.8.from_fold_ref.static_fold_ref = f32[64,128]{1,0:T(8,128)S(1)} collective-permute-done((f32[64,128]{1,0:T(8,128)S(1)}, f32[64,128]{1,0:T(8,128)S(1)}, u32[]{:S(2)}, u32[]{:S(2)}) %collective-permute-start.8) | collective-permute-done | bytes 32800 | tf_op jit(solution)/shard_map/ppermute | solution.py:730
  34.7 0.0 copy-done.1
  34.7 2.4 %shard_map.108 = (f32[16,64,256]{2,1,0:T(8,128)S(1)}, f32[8,64,256]{2,1,0:T(8,128)S(1)}) custom-call(f32[16,64,256]{2,1,0:T(8,128)S(1)} %bitcast.3, f32[64,128]{1,0:T(8,128)S(1)} %collective-permute-done.6.from_far_ref.static_far_ref, f32[64,128]{1,0:T(8,128)S(1)} %collective-permute-done.7.from_near_ref.static_near_ref, ...), custom_call_target="tpu_custom_call" | custom-call | bytes 8000000 | tf_op jit(solution)/shard_map/pallas_call | solution.py:50
  37.1 0.0 collective-permute-done.5.helped_ref
  37.2 1.3 %shard_map.109 = (f32[16,64,256]{2,1,0:T(8,128)S(1)}, f32[8,64,256]{2,1,0:T(8,128)}, f32[2,64,256]{2,1,0:T(8,128)S(1)}, f32[64,128]{1,0:T(8,128)S(1)}, f32[64,12...) custom-call(f32[512,256]{1,0:T(8,128)S(1)} %shard_map.107.total_ref, ...), custom_call_target="tpu_custom_call" | custom-call | bytes 4000000 | tf_op jit(solution)/shard_map/pallas_call | solution.py:50
  38.5 1.4 %collective-permute-start.9 = (f32[64,128]{1,0:T(8,128)S(1)}, f32[64,128]{1,0:T(8,128)S(1)}, u32[]{:S(2)}, u32[]{:S(2)}) collective-permute-start(f32[64,128]{1,0:T(8,128)S(1)} %get-tuple-element.32), channel_id=1, source_target_pairs={{0,112},{16,32},{32,16},{48,64},{64,48},{80,96},{96,80},{112,0},{1... | collective-permute-start | bytes 98312 | tf_op jit(solution)/shard_map/ppermute | solution.py:654
  39.8 0.0 collective-permute-start.10
  39.8 0.0 collective-permute-start.11
  39.8 5.6 %collective-permute-start.12 = (f32[64,128]{1,0:T(8,128)S(1)}, f32[64,128]{1,0:T(8,128)S(1)}, u32[]{:S(2)}, u32[]{:S(2)}) collective-permute-start(f32[64,128]{1,0:T(8,128)S(1)} %get-tuple-element.35), channel_id=1, source_target_pairs={{1,2},{2,1},{3,4},{4,3},{5,6},{6,5},{7,8},{8,7},{9,10},{10,9},{11,... | collective-permute-start | bytes 98312 | tf_op jit(solution)/shard_map/ppermute | solution.py:648
  45.5 0.0 collective-permute-done.9.from_far_ref
  45.5 0.0 collective-permute-done.10.from_near_ref
  45.5 0.0 collective-permute-done.11.from_sibling_ref
  45.5 2.6 %collective-permute-done.12.from_other_ref.from_fold_ref = f32[64,128]{1,0:T(8,128)S(1)} collective-permute-done((f32[64,128]{1,0:T(8,128)S(1)}, f32[64,128]{1,0:T(8,128)S(1)}, u32[]{:S(2)}, u32[]{:S(2)}) %collective-permute-start.12) | collective-permute-done | bytes 32800 | tf_op jit(solution)/shard_map/ppermute | solution.py:648
  48.1 3.1 %shard_map.110 = f32[16,64,256]{2,1,0:T(8,128)} custom-call(f32[16,64,256]{2,1,0:T(8,128)S(1)} %get-tuple-element.31.q_ref, f32[64,128]{1,0:T(8,128)S(1)} %collective-permute-done.9.from_far_ref, f32[64,128]{1,0:T(8,128)S(1)} %collective-permute-done.10.from_near_ref, f32[64,128]{1,0:T(8,128)S(1)} %collective-permute-done.11.from_sibling_ref, ...), custom_call_target="tpu_custom_call" | custom-call | bytes 8000000 | tf_op jit(solution)/shard_map/pallas_call | solution.py:50
  (9 shorter events, 0.0 us)
Async XLA Ops:
  0.6 8.6 %copy-start.3 = (s32[512,128]{1,0:T(8,128)S(1)}, s32[512,128]{1,0:T(8,128)}, u32[]{:S(2)}) copy-start(s32[512,128]{1,0:T(8,128)} %refs_0_.3) | copy-start | bytes 786436
  0.6 8.6 %copy-start.4 = (s32[512,128]{1,0:T(8,128)S(1)}, s32[512,128]{1,0:T(8,128)}, u32[]{:S(2)}) copy-start(s32[512,128]{1,0:T(8,128)} %refs_1_.5) | copy-start | bytes 786436
  0.7 8.6 %copy-start.5 = (f32[512,128]{1,0:T(8,128)S(1)}, f32[512,128]{1,0:T(8,128)}, u32[]{:S(2)}) copy-start(f32[512,128]{1,0:T(8,128)} %refs_2_.5) | copy-start | bytes 786436
  0.7 8.6 %copy-start.8 = (f32[8,16,128]{2,1,0:T(8,128)S(1)}, f32[8,16,128]{2,1,0:T(8,128)}, u32[]{:S(2)}) copy-start(f32[8,16,128]{2,1,0:T(8,128)} %refs_3_.5) | copy-start | bytes 196612
  3.9 5.3 %collective-permute-start = (f32[384,128]{1,0:T(8,128)}, f32[384,128]{1,0:T(8,128)S(1)}, u32[]{:S(2)}, u32[]{:S(2)}) collective-permute-start(f32[384,128]{1,0:T(8,128)} %get-tuple-element.20), channel_id=1, source_target_pairs={{0,1},{1,0},{2,3},{3,2},{4,5},{5,4},{6,7},{7,6},{8,9},{9,8},{10,11... | collective-permute-start | bytes 589832 | tf_op jit(solution)/shard_map/ppermute | solution.py:656
  4.6 9.7 %collective-permute-start.1 = (f32[384,128]{1,0:T(8,128)}, f32[384,128]{1,0:T(8,128)S(1)}, u32[]{:S(2)}, u32[]{:S(2)}) collective-permute-start(f32[384,128]{1,0:T(8,128)} %get-tuple-element.21), channel_id=1, source_target_pairs={{1,2},{2,1},{3,4},{4,3},{5,6},{6,5},{7,8},{8,7},{9,10},{10,9},{11,... | collective-permute-start | bytes 589832 | tf_op jit(solution)/shard_map/ppermute | solution.py:651
  5.3 8.5 %collective-permute-start.2 = (f32[224,128]{1,0:T(8,128)}, f32[224,128]{1,0:T(8,128)S(1)}, u32[]{:S(2)}, u32[]{:S(2)}) collective-permute-start(f32[224,128]{1,0:T(8,128)} %get-tuple-element.22), channel_id=1, source_target_pairs={{7,14},{8,15},{10,12},{9,11},{23,30},{24,31},{26,28},{25,27},{39,4... | collective-permute-start | bytes 344072 | tf_op jit(solution)/shard_map/ppermute | solution.py:712
  6.6 7.7 %collective-permute-start.3 = (f32[224,128]{1,0:T(8,128)}, f32[224,128]{1,0:T(8,128)S(1)}, u32[]{:S(2)}, u32[]{:S(2)}) collective-permute-start(f32[224,128]{1,0:T(8,128)} %get-tuple-element.23), channel_id=1, source_target_pairs={{8,14},{7,15},{24,30},{23,31},{40,46},{39,47},{56,62},{55,63},{72,... | collective-permute-start | bytes 344072 | tf_op jit(solution)/shard_map/ppermute | solution.py:712
  7.9 6.4 %collective-permute-start.4 = (f32[224,128]{1,0:T(8,128)}, f32[224,128]{1,0:T(8,128)S(1)}, u32[]{:S(2)}, u32[]{:S(2)}) collective-permute-start(f32[224,128]{1,0:T(8,128)} %get-tuple-element.24), channel_id=1, source_target_pairs={{9,14},{13,15},{25,30},{29,31},{41,46},{45,47},{57,62},{61,63},{73... | collective-permute-start | bytes 344072 | tf_op jit(solution)/shard_map/ppermute | solution.py:712
  13.1 2.8 %copy-start.11 = (f32[64,128]{1,0:T(8,128)S(1)}, f32[64,128]{1,0:T(8,128)}, u32[]{:S(2)}) copy-start(f32[64,128]{1,0:T(8,128)} %get-tuple-element.25) | copy-start | bytes 98308
  13.1 7.8 %copy-start.10 = (f32[64,128]{1,0:T(8,128)S(1)}, f32[64,128]{1,0:T(8,128)}, u32[]{:S(2)}) copy-start(f32[64,128]{1,0:T(8,128)} %get-tuple-element.26) | copy-start | bytes 98308
  14.3 12.0 %copy-start.9 = (f32[64,128]{1,0:T(8,128)S(1)}, f32[64,128]{1,0:T(8,128)}, u32[]{:S(2)}) copy-start(f32[64,128]{1,0:T(8,128)} %get-tuple-element.28) | copy-start | bytes 98308
  14.6 22.5 %collective-permute-start.5 = (f32[512,256]{1,0:T(8,128)S(1)}, f32[512,256]{1,0:T(8,128)S(1)}, u32[]{:S(2)}, u32[]{:S(2)}) collective-permute-start(f32[512,256]{1,0:T(8,128)S(1)} %shard_map.106.refs_9_.more_refs_0_), channel_id=1, source_target_pairs={{12,14},{11,15},{28,30},{27,31},{44,46},{43,47},{60,62},{59,63},{7... | collective-permute-start | bytes 1572872 | tf_op jit(solution)/shard_map/ppermute | solution.py:721
  15.9 13.7 %collective-permute-start.6 = (f32[64,128]{1,0:T(8,128)S(1)}, f32[64,128]{1,0:T(8,128)S(1)}, u32[]{:S(2)}, u32[]{:S(2)}) collective-permute-start(f32[64,128]{1,0:T(8,128)S(1)} %copy-done.11), channel_id=1, source_target_pairs={{0,112},{16,32},{32,16},{48,64},{64,48},{80,96},{96,80},{112,0},{1... | collective-permute-start | bytes 98312 | tf_op jit(solution)/shard_map/ppermute | solution.py:654
  20.9 13.8 %copy-start = (f32[8,64,256]{2,1,0:T(8,128)S(1)}, f32[8,64,256]{2,1,0:T(8,128)}, u32[]{:S(2)}) copy-start(f32[8,64,256]{2,1,0:T(8,128)} %east_ref.3) | copy-start | bytes 1572868
  20.9 13.8 %copy-start.1 = (f32[8,64,256]{2,1,0:T(8,128)S(1)}, f32[8,64,256]{2,1,0:T(8,128)}, u32[]{:S(2)}) copy-start(f32[8,64,256]{2,1,0:T(8,128)} %north_ref.3) | copy-start | bytes 1572868
  20.9 13.8 %copy-start.2 = (f32[2,8,64,256]{3,2,1,0:T(8,128)S(1)}, f32[2,8,64,256]{3,2,1,0:T(8,128)}, u32[]{:S(2)}) copy-start(f32[2,8,64,256]{3,2,1,0:T(8,128)} %param.9) | copy-start | bytes 3145732
  20.9 13.8 %copy-start.6 = (f32[7,64,256]{2,1,0:T(8,128)S(1)}, f32[7,64,256]{2,1,0:T(8,128)}, u32[]{:S(2)}) copy-start(f32[7,64,256]{2,1,0:T(8,128)} %mix_ref.3) | copy-start | bytes 1376260
  20.9 13.8 %copy-start.7 = (s32[64,256]{1,0:T(8,128)S(1)}, s32[64,256]{1,0:T(8,128)}, u32[]{:S(2)}) copy-start(s32[64,256]{1,0:T(8,128)} %count_ref.3) | copy-start | bytes 196612
  21.0 8.7 %collective-permute-start.7 = (f32[64,128]{1,0:T(8,128)S(1)}, f32[64,128]{1,0:T(8,128)S(1)}, u32[]{:S(2)}, u32[]{:S(2)}) collective-permute-start(f32[64,128]{1,0:T(8,128)S(1)} %copy-done.10), channel_id=1, source_target_pairs={{0,16},{16,0},{32,48},{48,32},{64,80},{80,64},{96,112},{112,96},{1... | collective-permute-start | bytes 98312 | tf_op jit(solution)/shard_map/ppermute | solution.py:655
  26.4 8.3 %collective-permute-start.8 = (f32[64,128]{1,0:T(8,128)S(1)}, f32[64,128]{1,0:T(8,128)S(1)}, u32[]{:S(2)}, u32[]{:S(2)}) collective-permute-start(f32[64,128]{1,0:T(8,128)S(1)} %copy-done.9), channel_id=1, source_target_pairs={{15,127},{31,111},{47,95},{63,79},{79,63},{95,47},{111,31},{127,15}} | collective-permute-start | bytes 98312 | tf_op jit(solution)/shard_map/ppermute | solution.py:730
  38.5 7.0 %collective-permute-start.9 = (f32[64,128]{1,0:T(8,128)S(1)}, f32[64,128]{1,0:T(8,128)S(1)}, u32[]{:S(2)}, u32[]{:S(2)}) collective-permute-start(f32[64,128]{1,0:T(8,128)S(1)} %get-tuple-element.32), channel_id=1, source_target_pairs={{0,112},{16,32},{32,16},{48,64},{64,48},{80,96},{96,80},{112,0},{1... | collective-permute-start | bytes 98312 | tf_op jit(solution)/shard_map/ppermute | solution.py:654
  39.8 5.6 %collective-permute-start.10 = (f32[64,128]{1,0:T(8,128)S(1)}, f32[64,128]{1,0:T(8,128)S(1)}, u32[]{:S(2)}, u32[]{:S(2)}) collective-permute-start(f32[64,128]{1,0:T(8,128)S(1)} %get-tuple-element.33), channel_id=1, source_target_pairs={{0,16},{16,0},{32,48},{48,32},{64,80},{80,64},{96,112},{112,96},{1... | collective-permute-start | bytes 98312 | tf_op jit(solution)/shard_map/ppermute | solution.py:655
  39.8 5.7 %collective-permute-start.11 = (f32[64,128]{1,0:T(8,128)S(1)}, f32[64,128]{1,0:T(8,128)S(1)}, u32[]{:S(2)}, u32[]{:S(2)}) collective-permute-start(f32[64,128]{1,0:T(8,128)S(1)} %get-tuple-element.34), channel_id=1, source_target_pairs={{0,1},{1,0},{2,3},{3,2},{4,5},{5,4},{6,7},{7,6},{8,9},{9,8},{10,11... | collective-permute-start | bytes 98312 | tf_op jit(solution)/shard_map/ppermute | solution.py:656
  39.8 8.3 %collective-permute-start.12 = (f32[64,128]{1,0:T(8,128)S(1)}, f32[64,128]{1,0:T(8,128)S(1)}, u32[]{:S(2)}, u32[]{:S(2)}) collective-permute-start(f32[64,128]{1,0:T(8,128)S(1)} %get-tuple-element.35), channel_id=1, source_target_pairs={{1,2},{2,1},{3,4},{4,3},{5,6},{6,5},{7,8},{8,7},{9,10},{10,9},{11,... | collective-permute-start | bytes 98312 | tf_op jit(solution)/shard_map/ppermute | solution.py:648
